TPU v7x, 32 devices: a whole 2x2x4 slice. The times are simulated.
32 devices in a mesh: groups: 2 (over y), expert: 16 (over z, x, core).
Axes of the slice: x: 2, y: 2, z: 4, core: 2. Of those that a mesh axis runs over, the one named last changes fastest.
Arguments:
- tokens: bfloat16 [4096, 1024], P(('groups', 'expert')), parts along dimension 0, may hold values from -6 to 6
- segments: int32 [32, 128], P(('groups', 'expert')), parts along dimension 0, may hold values from 0 to 3, never falling along the last dimension, each value on 1 to 64 neighbouring positions
- lengths: int32 [32], P(('groups', 'expert')), parts along dimension 0, may hold values from 32 to 128
- attn_gain: float32 [1024], replicated, may hold values from 0.1 to 1.9
- attn_weight: bfloat16 [1024, 4096], P(None, 'expert'), may hold values from -0.1875 to 0.1875
- ffn_gain: float32 [1024], replicated, may hold values from 0.1 to 1.9
- routes: int32 [4096, 2], P(('groups', 'expert')), parts along dimension 0, may hold values from 0 to 7, all different within a row; in each aligned block of 128 rows (0 to 127, 128 to 255, ...) at most 40 rows name the same one
- route_gates: float32 [4096, 2], P(('groups', 'expert')), parts along dimension 0, may hold values from 0.2 to 1
- expert_in: bfloat16 [16, 1024, 2048], P('expert'), may hold values from -0.1875 to 0.1875
- expert_out: bfloat16 [16, 2048, 1024], P('expert'), may hold values from -0.09375 to 0.09375
- teacher: float32 [32, 4, 1024], P(('groups', 'expert')), parts along dimension 0, may hold values from -6 to 6
Outputs:
- grad_tokens: bfloat16 [4096, 1024], P(('groups', 'expert')), parts along dimension 0
- pooled: float32 [32, 4, 1024], P(('groups', 'expert')), parts along dimension 0
There are 2 independent parts, one for each index of `groups`. A program takes and returns all parts, laid end to end along the dimension named above; an argument that names none is the same for every part. Nothing has to cross between parts.
Inputs may be any that keep to these rules, and one draw needn't show every extreme that they name: `routes`: each token names two different experts; among the 128 tokens of one device no expert is named more than 40 times. `segments`: within a row segment numbers never fall, and each of the 4 sentences holds 1 to 64 positions.
All inputs are finite; a program needn't handle non-finite values.
Results may differ from a plain program's by a relative error of at most 0.029.
The roundings to bfloat16 on the way count: a program that leaves them out, or rounds other values in their place, can miss the bound.
Values may be sent and summed in bfloat16 or wider, within the bound.
A program may use at most 128 MiB of HBM per device.

v0:
```python
import jax
import jax.numpy as jnp
from jax import lax
from jax.sharding import PartitionSpec as P

HEADS = 8
SPLIT = 2


epsilon = 1e-05


def layer_norm(inputs, scale_gain):
    average = jnp.mean(inputs, axis=-1, keepdims=True)
    centred = inputs - average
    variance = jnp.mean(centred * centred, axis=-1, keepdims=True)
    return centred * lax.rsqrt(variance + epsilon) * scale_gain


def key_allowed(segments, lengths):
    positions = jnp.arange(segments.shape[1], dtype=jnp.int32)
    same_seg = segments[:, :, None] == segments[:, None, :]
    key_live = positions[None, None, :] < lengths[:, None, None]
    itself = positions[:, None] == positions[None, :]
    return jnp.logical_or(jnp.logical_and(same_seg, key_live), itself[None])


def attend(inputs, weight, allowed, scale_gain, head_count):
    row_count, length, model_width = inputs.shape
    head_width = model_width // head_count
    normed = (
        layer_norm(inputs, scale_gain).astype(jnp.bfloat16).reshape(row_count * length, model_width)
    )
    projected = jnp.dot(
        normed, weight[:, : 3 * model_width], preferred_element_type=jnp.float32
    ).astype(jnp.bfloat16)
    projected = projected.reshape(row_count, length, 3, head_count, head_width)
    queries = projected[:, :, 0]
    keys_all = projected[:, :, 1]
    values_all = projected[:, :, 2]
    scores = jnp.einsum(
        "rqhd,rkhd->rhqk", queries, keys_all, preferred_element_type=jnp.float32
    ) * head_width ** (-0.5)
    weights_exp = jnp.exp(scores) * allowed[:, None].astype(jnp.float32)
    probabilities = (weights_exp / jnp.sum(weights_exp, axis=-1, keepdims=True)).astype(
        jnp.bfloat16
    )
    context = jnp.einsum(
        "rhqk,rkhd->rqhd", probabilities, values_all, preferred_element_type=jnp.float32
    ).astype(jnp.bfloat16)
    context = context.reshape(row_count * length, model_width)
    output = jnp.dot(context, weight[:, 3 * model_width :], preferred_element_type=jnp.float32)
    return inputs + output.reshape(row_count, length, model_width)


def slot_places(block_routes, experts, capacity):
    flat_ids = block_routes.reshape(-1)
    onehot = (flat_ids[:, None] == jnp.arange(experts, dtype=jnp.int32)[None, :]).astype(jnp.int32)
    earlier = jnp.cumsum(onehot, axis=0, dtype=jnp.int32) - onehot
    position = jnp.sum(earlier * onehot, axis=1, dtype=jnp.int32)
    return flat_ids * capacity + position


def body(
    tokens,
    segments,
    lengths,
    attn_gain,
    attn_weight,
    ffn_gain,
    routes,
    route_gates,
    expert_in,
    expert_out,
    teacher,
):
    devices = lax.axis_size("expert")
    experts = devices // SPLIT
    tok_count, model_width = tokens.shape
    row_count, length = segments.shape
    seg_count = teacher.shape[1]
    capacity = max(2, 5 * tok_count // (2 * experts))
    allowed = key_allowed(segments, lengths)
    inputs = tokens.astype(jnp.float32).reshape(row_count, length, model_width)
    whole_weight = lax.all_gather(attn_weight, "expert", axis=1, tiled=True)
    hidden_state = attend(inputs, whole_weight, allowed, attn_gain, HEADS)
    hidden_flat = hidden_state.reshape(tok_count, model_width)

    def ffn_norm(source):
        return layer_norm(source, ffn_gain)

    normed_ffn, norm_pull = jax.vjp(ffn_norm, hidden_flat)
    normed_bf = normed_ffn.astype(jnp.bfloat16)
    slot_place = slot_places(routes, experts, capacity)
    slot_ids = jnp.arange(experts * capacity, dtype=jnp.int32)
    dispatch = (slot_ids[:, None] == slot_place[None, :]).astype(jnp.bfloat16)
    contract = (((1,), (1,)), ((), ()))

    def spread_pairs(packed):
        shaped = packed.reshape(experts, 1, capacity, model_width)
        return jnp.broadcast_to(shaped, (experts, SPLIT, capacity, model_width)).reshape(
            devices, capacity, model_width
        )

    def join_halves(returned):
        summed = jnp.sum(
            returned.reshape(experts, SPLIT, capacity, model_width).astype(jnp.float32), axis=1
        )
        picked = jnp.take(summed.reshape(experts * capacity, model_width), slot_place, axis=0)
        return picked.reshape(tok_count, 2, model_width)

    rows_rep = jnp.repeat(normed_bf, 2, axis=0)
    packed = jnp.dot(dispatch, rows_rep, preferred_element_type=jnp.float32).astype(jnp.bfloat16)
    arrived = lax.all_to_all(
        spread_pairs(packed), "expert", split_axis=0, concat_axis=0, tiled=True
    )
    pieces = arrived.shape[1]
    flat_rows = arrived.reshape(devices * pieces, model_width)
    activated = jnp.maximum(
        jnp.dot(flat_rows, expert_in[0], preferred_element_type=jnp.float32), 0.0
    ).astype(jnp.bfloat16)
    partial_out = jnp.dot(activated, expert_out[0], preferred_element_type=jnp.float32).astype(
        jnp.bfloat16
    )
    partial_out = partial_out.reshape(devices, pieces, model_width)
    returned = lax.all_to_all(partial_out, "expert", split_axis=0, concat_axis=0, tiled=True)
    returned, activated = (returned, activated.reshape(devices, pieces, activated.shape[1]))
    expert_sum = jnp.sum(join_halves(returned) * route_gates[:, :, None], axis=1)
    outputs = hidden_flat + expert_sum
    positions = jnp.arange(length, dtype=jnp.int32)
    live_mask = positions[None, :] < lengths[:, None]
    member_int = jnp.logical_and(
        segments[:, :, None] == jnp.arange(seg_count, dtype=jnp.int32)[None, None, :],
        live_mask[:, :, None],
    ).astype(jnp.int32)
    member = member_int.astype(jnp.float32)
    counts = jnp.sum(member_int, axis=1, dtype=jnp.int32)
    pooled = jnp.einsum(
        "rls,rld->rsd",
        member,
        outputs.reshape(row_count, length, model_width),
        precision=lax.Precision.HIGHEST,
    )
    pooled = pooled / jnp.maximum(counts, 1).astype(jnp.float32)[:, :, None]
    difference = pooled - teacher
    grad_out = jnp.einsum(
        "rls,rsd->rld", member, difference, precision=lax.Precision.HIGHEST
    ).reshape(tok_count, model_width)
    slot_grads = (
        (grad_out[:, None, :] * route_gates[:, :, None])
        .astype(jnp.bfloat16)
        .reshape(2 * tok_count, model_width)
    )
    grad_packed = jnp.dot(dispatch, slot_grads, preferred_element_type=jnp.float32).astype(
        jnp.bfloat16
    )
    grad_arrived = lax.all_to_all(
        spread_pairs(grad_packed), "expert", split_axis=0, concat_axis=0, tiled=True
    )
    flat_grads = grad_arrived.reshape(devices * capacity, model_width)
    act_flat = activated.reshape(devices * capacity, activated.shape[2])
    product = lax.dot_general(
        flat_grads, expert_out[0], contract, preferred_element_type=jnp.float32
    )
    grad_pre = jnp.where(act_flat > 0, product, 0.0).astype(jnp.bfloat16)
    grad_part = lax.dot_general(
        grad_pre, expert_in[0], contract, preferred_element_type=jnp.float32
    ).astype(jnp.bfloat16)
    grad_back = lax.all_to_all(
        grad_part.reshape(devices, capacity, model_width),
        "expert",
        split_axis=0,
        concat_axis=0,
        tiled=True,
    )
    grad_normed = jnp.sum(join_halves(grad_back), axis=1)
    grad_hidden = (grad_out + norm_pull(grad_normed)[0]).reshape(row_count, length, model_width)
    again_weight = lax.all_gather(attn_weight, "expert", axis=1, tiled=True)

    def attention_again(source):
        return attend(source, again_weight, allowed, attn_gain, HEADS)

    grad_inputs = jax.vjp(attention_again, inputs)[1](grad_hidden)[0]
    grad_tokens = grad_inputs.reshape(tok_count, model_width).astype(jnp.bfloat16)
    return (grad_tokens, pooled)


def solution(mesh):
    placed = (
        P(("groups", "expert"), None),
        P(("groups", "expert"), None),
        P(("groups", "expert")),
        P(),
        P(None, "expert"),
        P(),
        P(("groups", "expert"), None),
        P(("groups", "expert"), None),
        P("expert", None, None),
        P("expert", None, None),
        P(("groups", "expert"), None, None),
    )
    return jax.shard_map(
        body,
        mesh=mesh,
        in_specs=placed,
        out_specs=(P(("groups", "expert"), None), P(("groups", "expert"), None, None)),
        check_vma=False,
    )
```

profile of v0, /device:TPU:0, one launch (start us, length us, event | category | flops | bytes accessed | tf_op | source)
XLA Modules:
  0.0 289.0 jit_solution(10185929232018740254)
XLA Ops:
  7.2 0.7 all-gather.2.cloned.1.call-update
  7.9 0.8 copy.59
  9.6 0.6 reduce-window.6
  10.6 1.1 convert_reduce_fusion.2
  11.7 1.2 fusion.59
  12.8 0.8 fusion.74
  13.7 77.3 %all-gather.2.cloned.1.call-done = bf16[1024,4096]{1,0:T(8,128)(2,1)} async-done(((bf16[1024,256]{1,0:T(8,128)(2,1)}), bf16[1024,4096]{1,0:T(8,128)(2,1)}) %all-gather.2.cloned.1.call-update) | async-done | bytes 8388624 | tf_op jit(solution)/shard_map/all_gather | solution.py:85
  91.0 4.0 %fusion.29 = bf16[16,8,24,128]{3,1,2,0:T(8,128)(2,1)S(1)} fusion(bf16[1024,4096]{1,0:T(8,128)(2,1)} %all-gather.2.cloned.1.call-done, bf16[128,1024]{1,0:T(8,128)(2,1)} %param.13, f32[1024]{0:T(1024)} %param.16, f32[128]{0:T(128)S(1)} %fusion.95, f32[128]{0:T(128)S(1)} %broadcast_multiply_fusion.1), kind=kOutput, calls=%fused_computation.27 | convolution fusion | flops 806354944 | bytes 7345152 | tf_op jit(solution)/shard_map/dot_general | solution.py:34
  96.7 2.1 fusion.102
  100.2 34.6 %all_to_all.20 = bf16[16,40,1024]{2,1,0:T(8,128)(2,1)S(1)} all-to-all(bf16[16,40,1024]{2,1,0:T(8,128)(2,1)S(1)} %bitcast.117), channel_id=1, replica_groups=mesh['groups'=2,'expert'=16] {'expert'}, dimensions={0} | all-to-all | bytes 2621440 | tf_op jit(solution)/shard_map/all_to_all | solution.py:114
  134.8 3.1 %maximum_convert_fusion = bf16[640,2048]{1,0:T(8,128)(2,1)S(1)} fusion(bf16[640,1024]{1,0:T(8,128)(2,1)S(1)} %bitcast.123, bf16[1,1024,2048]{2,1,0:T(8,128)(2,1)S(1)} %copy-done.14), kind=kOutput, calls=%fused_computation.7 | convolution fusion | flops 2686976000 | bytes 8126464 | tf_op jit(solution)/shard_map/dot_general | solution.py:120
  138.0 4.0 %fusion.26 = bf16[640,1024]{1,0:T(8,128)(2,1)} fusion(bf16[640,2048]{1,0:T(8,128)(2,1)S(1)} %maximum_convert_fusion, bf16[1,2048,1024]{2,1,0:T(8,128)(2,1)S(1)} %copy-done.15), kind=kOutput, calls=%fused_computation.24 | convolution fusion | flops 2685009920 | bytes 8126464 | tf_op jit(solution)/shard_map/dot_general | solution.py:122
  142.0 4.7 %all-to-all-start.1 = ((bf16[16,40,1024]{2,1,0:T(8,128)(2,1)}), bf16[16,40,1024]{2,1,0:T(8,128)(2,1)}, u32[]{:S(2)}, u32[]{:S(2)}) async-start(bf16[16,40,1024]{2,1,0:T(8,128)(2,1)} %bitcast.16), calls=%async_computation.1 | async-start | bytes 2621440 | tf_op jit(solution)/shard_map/all_to_all | solution.py:126
  147.1 26.8 %all-to-all-done.1 = bf16[16,40,1024]{2,1,0:T(8,128)(2,1)} async-done(((bf16[16,40,1024]{2,1,0:T(8,128)(2,1)}), bf16[16,40,1024]{2,1,0:T(8,128)(2,1)}, u32[]{:S(2)}, u32[]{:S(2)}) %all-to-all-start.1) | async-done | bytes 1310752 | tf_op jit(solution)/shard_map/all_to_all | solution.py:126
  173.9 1.7 convert_reduce_fusion.1
  175.7 1.1 gather_fusion
  176.9 0.6 reshape.582
  177.5 1.3 multiply_reduce_fusion
  179.3 0.6 fusion.75
  180.3 0.7 mul.234
  181.6 39.3 %all_to_all.21 = bf16[16,40,1024]{2,1,0:T(8,128)(2,1)S(1)} all-to-all(bf16[16,40,1024]{2,1,0:T(8,128)(2,1)S(1)} %bitcast.118), channel_id=1, replica_groups=mesh['groups'=2,'expert'=16] {'expert'}, dimensions={0} | all-to-all | bytes 2621440 | tf_op jit(solution)/shard_map/all_to_all | solution.py:157
  220.9 10.8 %fusion.23 = bf16[640,1024]{1,0:T(8,128)(2,1)} fusion(bf16[1,1024,2048]{2,1,0:T(8,128)(2,1)} %param.21, bf16[640,2048]{1,0:T(8,128)(2,1)} %copy-done.17, bf16[640,1024]{1,0:T(8,128)(2,1)S(1)} %bitcast.122, bf16[1,2048,1024]{2,1,0:T(8,128)(2,1)} %param.22), kind=kOutput, calls=%fused_computation.23 | convolution fusion | flops 5373296640 | bytes 13631488 | tf_op jit(solution)/shard_map/dot_general | solution.py:166
  231.7 4.6 %all-to-all-start.3 = ((bf16[16,40,1024]{2,1,0:T(8,128)(2,1)}), bf16[16,40,1024]{2,1,0:T(8,128)(2,1)}, u32[]{:S(2)}, u32[]{:S(2)}) async-start(bf16[16,40,1024]{2,1,0:T(8,128)(2,1)} %bitcast.24), calls=%async_computation.3 | async-start | bytes 2621440 | tf_op jit(solution)/shard_map/all_to_all | solution.py:169
  236.4 27.2 %all-to-all-done.3 = bf16[16,40,1024]{2,1,0:T(8,128)(2,1)} async-done(((bf16[16,40,1024]{2,1,0:T(8,128)(2,1)}), bf16[16,40,1024]{2,1,0:T(8,128)(2,1)}, u32[]{:S(2)}, u32[]{:S(2)}) %all-to-all-start.3) | async-done | bytes 1310752 | tf_op jit(solution)/shard_map/all_to_all | solution.py:169
  263.5 1.7 convert_reduce_fusion
  265.3 2.1 gather_fusion.1
  267.4 1.4 broadcast_select_fusion
  268.7 0.6 reshape.588
  269.4 1.2 reduce_sum.156
  271.1 2.5 fusion.36
  275.8 5.1 %fusion.62 = (f32[128]{0:T(128)S(1)}, f32[128,1024]{1,0:T(8,128)S(1)}) fusion(bf16[128,1024]{1,0:T(8,128)(2,1)S(1)} %copy-done, f32[128]{0:T(128)S(1)} %broadcast_multiply_fusion.1, f32[1024]{0:T(1024)S(1)} %copy-done.16, bf16[128,3072]{0,1:T(8,128)(2,1)S(1)} %bitcast.126, bf16[1024,4096]{1,0:T(8,128)(2,1)} %all-gather.2.cloned.1.call-done), kind=kOutput, calls=%fused_computation.60 | convolution fusion | flops 806223744 | bytes 7869440 | tf_op jit(solution)/shard_map/transpose(jvp())/dot_general | solution.py:34
  281.2 1.0 add_convert_fusion
  (87 shorter events, 8.4 us)
Async XLA Ops:
  7.2 83.8 %all-gather.2.cloned.1.call-start = ((), (), s32[]{:S(2)}) async-start(), calls=%async_computation.4 | async-start | bytes 8912896 | tf_op jit(solution)/shard_map/all_gather | solution.py:85
  95.1 1.5 copy-start
  95.3 3.5 %copy-start.5 = (bf16[1,128,1,8,128]{4,3,2,1,0:T(8,128)(2,1)}, bf16[1,128,1,8,128]{4,3,2,1,0:T(8,128)(2,1)S(1)}, u32[]{:S(2)}) copy-start(bf16[1,128,1,8,128]{4,3,2,1,0:T(8,128)(2,1)S(1)} %get-tuple-element.8) | copy-start | bytes 786436
  95.3 3.5 %copy-start.7 = (bf16[1,128,1,8,128]{4,3,2,1,0:T(8,128)(2,1)}, bf16[1,128,1,8,128]{4,3,2,1,0:T(8,128)(2,1)S(1)}, u32[]{:S(2)}) copy-start(bf16[1,128,1,8,128]{4,3,2,1,0:T(8,128)(2,1)S(1)} %get-tuple-element.9) | copy-start | bytes 786436
  95.5 0.7 copy-start.1
  95.9 0.8 copy-start.3
  95.9 3.2 %copy-start.10 = (f32[1024]{0:T(1024)S(1)}, f32[1024]{0:T(1024)}, u32[]{:S(2)}) copy-start(f32[1024]{0:T(1024)} %param.18) | copy-start | bytes 12292
  99.7 35.1 %copy-start.14 = (bf16[1,1024,2048]{2,1,0:T(8,128)(2,1)S(1)}, bf16[1,1024,2048]{2,1,0:T(8,128)(2,1)}, u32[]{:S(2)}) copy-start(bf16[1,1024,2048]{2,1,0:T(8,128)(2,1)} %param.21) | copy-start | bytes 12582916
  134.8 3.1 %copy-start.15 = (bf16[1,2048,1024]{2,1,0:T(8,128)(2,1)S(1)}, bf16[1,2048,1024]{2,1,0:T(8,128)(2,1)}, u32[]{:S(2)}) copy-start(bf16[1,2048,1024]{2,1,0:T(8,128)(2,1)} %param.22) | copy-start | bytes 12582916
  137.9 4.1 %copy-start.17 = (bf16[640,2048]{1,0:T(8,128)(2,1)}, bf16[640,2048]{1,0:T(8,128)(2,1)S(1)}, u32[]{:S(2)}) copy-start(bf16[640,2048]{1,0:T(8,128)(2,1)S(1)} %maximum_convert_fusion) | copy-start | bytes 7864324
  142.0 4.7 %copy-start.13 = (f32[128,2]{0,1:T(2,128)S(1)}, f32[128,2]{0,1:T(2,128)}, u32[]{:S(2)}) copy-start(f32[128,2]{0,1:T(2,128)} %param.20) | copy-start | bytes 3076
  142.0 5.0 %copy-start.12 = (s32[1,128]{1,0:T(1,128)S(1)}, s32[1,128]{1,0:T(1,128)}, u32[]{:S(2)}) copy-start(s32[1,128]{1,0:T(1,128)} %param.14) | copy-start | bytes 1540
  142.0 31.9 %all-to-all-start.1 = ((bf16[16,40,1024]{2,1,0:T(8,128)(2,1)}), bf16[16,40,1024]{2,1,0:T(8,128)(2,1)}, u32[]{:S(2)}, u32[]{:S(2)}) async-start(bf16[16,40,1024]{2,1,0:T(8,128)(2,1)} %bitcast.16), calls=%async_computation.1 | async-start | bytes 2621440 | tf_op jit(solution)/shard_map/all_to_all | solution.py:126
  176.9 2.4 copy-start.11
  179.3 2.2 copy-start.9
  231.7 31.8 %all-to-all-start.3 = ((bf16[16,40,1024]{2,1,0:T(8,128)(2,1)}), bf16[16,40,1024]{2,1,0:T(8,128)(2,1)}, u32[]{:S(2)}, u32[]{:S(2)}) async-start(bf16[16,40,1024]{2,1,0:T(8,128)(2,1)} %bitcast.24), calls=%async_computation.3 | async-start | bytes 2621440 | tf_op jit(solution)/shard_map/all_to_all | solution.py:169
  270.8 2.9 %copy-start.4 = (f32[8,128,128]{1,2,0:T(8,128)S(1)}, f32[8,128,128]{1,2,0:T(8,128)}, u32[]{:S(2)}) copy-start(f32[8,128,128]{1,2,0:T(8,128)} %copy-done.3) | copy-start | bytes 1572868
  271.1 3.0 %copy-start.2 = (bf16[1,128,1,8,128]{1,4,3,2,0:T(8,128)(2,1)S(1)}, bf16[1,128,1,8,128]{1,4,3,2,0:T(8,128)(2,1)}, u32[]{:S(2)}) copy-start(bf16[1,128,1,8,128]{1,4,3,2,0:T(8,128)(2,1)} %copy-done.1) | copy-start | bytes 786436
  273.6 1.0 copy-start.8
  274.1 1.0 copy-start.6
  275.1 0.7 copy-start.16
Sparse Core Ops, SparseCore 0:
  10.1 80.7 all-gather.1
where the time goes:
time: 292 us; the launch traced here: 289 us
  waiting for transfers between devices  132 us (45%)
  blocking collectives  73.9 us (25%)
  matrix products  35.2 us (12%)
  between operations  15.2 us (5%)
  other arithmetic  13.7 us (5%)
  local copies, waits for them, and re-layouts  9.75 us (3%)
  starting transfers between devices  9.36 us (3%)
    all_gather x1, waiting for transfers between devices, body(): whole_weight = lax.all_gather(attn_weight, 'expert', axis=1, tiled=True)  77.3 us
    all_to_all x1, blocking collectives, body(): lax.all_to_all(spread_pairs(grad_packed), 'expert', split_axis=0, concat_...  39.3 us
    all_to_all x1, blocking collectives, body(): lax.all_to_all(spread_pairs(packed), 'expert', split_axis=0, concat_axis=...  34.6 us
    all_to_all x1, waiting for transfers between devices, body(): lax.all_to_all(grad_part.reshape(devices, capacity, model_width), 'expert...  27.2 us
    all_to_all x1, waiting for transfers between devices, body(): lax.all_to_all(partial_out, 'expert', split_axis=0, concat_axis=0, tiled=...  26.8 us
    dot_general x1, matrix products, body(): lax.dot_general(grad_pre, expert_in[0], contract, preferred_element_type=...  10.8 us
    dot_general x2, matrix products, attend(): jnp.dot(normed, weight[:, :3 * model_width], preferred_element_type=jnp.f...  9.07 us
  transfers between devices with their start and end apart: 3, of which 3 were waited for; matrix products, arithmetic and copies ran while one was open for 2% of the time, Pallas kernels for 0%

commit v1 on v0

--- a/solution.py
+++ b/solution.py
@@ -1,10 +1,17 @@
+import functools
+
 import jax
 import jax.numpy as jnp
 from jax import lax
+from jax.experimental import pallas as pl
+from jax.experimental.pallas import tpu as pltpu
 from jax.sharding import PartitionSpec as P
 
 HEADS = 8
 SPLIT = 2
+MESH = pl.DeviceIdType.MESH
+NT = (((1,), (1,)), ((), ()))
+TILE = 256
 
 
 epsilon = 1e-05
@@ -51,6 +58,187 @@
     context = context.reshape(row_count * length, model_width)
     output = jnp.dot(context, weight[:, 3 * model_width :], preferred_element_type=jnp.float32)
     return inputs + output.reshape(row_count, length, model_width)
+
+
+def flip(index, bits, count):
+    result, place = 0, 1
+    while place < count:
+        bit = lax.rem(lax.div(index, place), 2)
+        if (bits // place) % 2:
+            bit = 1 - bit
+        result = result + bit * place
+        place *= 2
+    return result
+
+
+def unfold(block):
+    wide = block.astype(jnp.float32)
+    cap = wide.shape[0] // 2
+    return jnp.concatenate([wide[:cap], wide[cap:]], axis=1)
+
+
+def fold(rows):
+    half = rows.shape[1] // 2
+    return jnp.concatenate([rows[:, :half], rows[:, half:]], axis=0)
+
+
+def expert_kernel(chips, backward, groups_of, *refs):
+    if backward:
+        packed, w1_hbm, w2_hbm, kept, out = refs[:5]
+        rest = refs[5:]
+    else:
+        packed, w1_hbm, w2_hbm, out, kept = refs[:5]
+        rest = refs[5:]
+    (w1, w2, got_a, got_b, x_ref, h_scr, part, to_pair, from_pair, to_back,
+     w_sem, send_a, recv_a, send_b, recv_b, send_c, recv_c, send_d, recv_d) = rest
+    rank = lax.axis_index("expert")
+    core = lax.rem(rank, 2)
+    chip = lax.div(rank, 2)
+    pair = 2 * chip + (1 - core)
+    cap = packed.shape[1] // 2
+    load_1 = pltpu.make_async_copy(w1_hbm.at[0], w1, w_sem.at[0])
+    load_2 = pltpu.make_async_copy(w2_hbm.at[0], w2, w_sem.at[1])
+    load_1.start()
+    load_2.start()
+    peer_chip = [flip(chip, k, chips) for k in range(chips)]
+    peer = [2 * peer_chip[k] + core for k in range(chips)]
+    barrier = pltpu.get_barrier_semaphore()
+    pl.semaphore_signal(barrier, inc=1, device_id={"expert": pair}, device_id_type=MESH)
+    for k in range(1, chips):
+        pl.semaphore_signal(barrier, inc=1, device_id={"expert": peer[k]}, device_id_type=MESH)
+    pl.semaphore_wait(barrier, chips)
+
+    def remote(src, dst, send, recv, target):
+        return pltpu.make_async_remote_copy(
+            src_ref=src, dst_ref=dst, send_sem=send, recv_sem=recv,
+            device_id={"expert": target}, device_id_type=MESH,
+        )
+
+    dispatch = {}
+    for k in range(chips - 1, 0, -1):
+        dispatch[k] = remote(packed.at[peer_chip[k]], got_a.at[k], send_a.at[k], recv_a.at[k], peer[k])
+        dispatch[k].start()
+    across, over, back = {}, {}, {}
+    across[0] = remote(packed.at[chip], got_b.at[0], send_b.at[0], recv_b.at[0], pair)
+    across[0].start()
+
+    w_ready = False
+    for group in groups_of:
+        for k in group:
+            if k:
+                dispatch[k].wait_recv()
+                across[k] = remote(got_a.at[k], got_b.at[k], send_b.at[k], recv_b.at[k], pair)
+                across[k].start()
+        for k in group:
+            across[k].wait_recv()
+            mine = got_a[k] if k else packed[chip]
+            rows = jnp.concatenate([unfold(mine), unfold(got_b[k])], axis=0)
+            x_ref[pl.ds(2 * cap * k, 2 * cap), :] = rows.astype(jnp.bfloat16)
+        if not w_ready:
+            load_1.wait()
+            load_2.wait()
+            w_ready = True
+        first, count = 2 * cap * group[0], 2 * cap * len(group)
+        block = pl.ds(first, count)
+        hidden = h_scr.shape[1]
+        width = part.shape[1]
+
+        def hidden_tile(j, carry):
+            columns = pl.ds(pl.multiple_of(j * TILE, TILE), TILE)
+            if backward:
+                value = lax.dot_general(
+                    x_ref[block, :], w2[columns, :], NT, preferred_element_type=jnp.float32
+                )
+                mask = kept[block, columns].astype(jnp.float32) > 0
+                h_scr[block, columns] = jnp.where(mask, value, 0.0).astype(jnp.bfloat16)
+            else:
+                value = jnp.dot(
+                    x_ref[block, :], w1[:, columns], preferred_element_type=jnp.float32
+                )
+                value = jnp.maximum(value, 0.0).astype(jnp.bfloat16)
+                h_scr[block, columns] = value
+                kept[block, columns] = value
+            return carry
+
+        lax.fori_loop(0, hidden // TILE, hidden_tile, 0)
+
+        def out_tile(j, carry):
+            columns = pl.ds(pl.multiple_of(j * TILE, TILE), TILE)
+            if backward:
+                part[block, columns] = lax.dot_general(
+                    h_scr[block, :], w1[columns, :], NT, preferred_element_type=jnp.float32
+                )
+            else:
+                part[block, columns] = jnp.dot(
+                    h_scr[block, :], w2[:, columns], preferred_element_type=jnp.float32
+                )
+            return carry
+
+        lax.fori_loop(0, width // TILE, out_tile, 0)
+        for k in group:
+            theirs = part[pl.ds(2 * cap * k + cap, cap), :]
+            to_pair[k] = fold(theirs).astype(jnp.bfloat16)
+            over[k] = remote(to_pair.at[k], from_pair.at[k], send_c.at[k], recv_c.at[k], pair)
+            over[k].start()
+        for k in reversed(group):
+            over[k].wait_recv()
+            total = fold(part[pl.ds(2 * cap * k, cap), :]) + from_pair[k].astype(jnp.float32)
+            if k:
+                to_back[k] = total.astype(jnp.bfloat16)
+                back[k] = remote(to_back.at[k], out.at[chip], send_d.at[k], recv_d.at[k], peer[k])
+                back[k].start()
+            else:
+                out[chip] = total.astype(jnp.bfloat16)
+    for k in range(chips):
+        if k:
+            dispatch[k].wait_send()
+            back[k].wait_send()
+            back[k].wait_recv()
+        across[k].wait_send()
+        over[k].wait_send()
+
+
+def run_experts(packed, expert_in, expert_out, kept=None):
+    chips, rows2, half = packed.shape
+    backward = kept is not None
+    rows = chips * rows2
+    width, hidden = expert_in.shape[1:]
+    groups_of = [list(range(chips // 2)), list(range(chips // 2, chips))]
+    vmem = pl.BlockSpec(memory_space=pltpu.VMEM)
+    hbm = pl.BlockSpec(memory_space=pl.ANY)
+    message = jax.ShapeDtypeStruct(packed.shape, jnp.bfloat16)
+    kept_shape = jax.ShapeDtypeStruct((rows, hidden), jnp.bfloat16)
+    block = pltpu.VMEM(packed.shape, jnp.bfloat16)
+    sems = pltpu.SemaphoreType.DMA((chips,))
+    return pl.pallas_call(
+        functools.partial(expert_kernel, chips, backward, groups_of),
+        out_shape=message if backward else (message, kept_shape),
+        in_specs=[vmem, hbm, hbm] + ([vmem] if backward else []),
+        out_specs=vmem if backward else (vmem, vmem),
+        scratch_shapes=[
+            pltpu.VMEM((width, hidden), jnp.bfloat16),
+            pltpu.VMEM((hidden, width), jnp.bfloat16),
+            block,
+            block,
+            pltpu.VMEM((rows, width), jnp.bfloat16),
+            pltpu.VMEM((rows, hidden), jnp.bfloat16),
+            pltpu.VMEM((rows, width), jnp.float32),
+            block,
+            block,
+            block,
+            pltpu.SemaphoreType.DMA((2,)),
+        ]
+        + [sems] * 8,
+        compiler_params=pltpu.CompilerParams(
+            collective_id=1 if backward else 0,
+            has_side_effects=True,
+            vmem_limit_bytes=44 * 1024 * 1024,
+        ),
+        cost_estimate=pl.CostEstimate(
+            flops=4 * rows * width * hidden, bytes_accessed=20 * 2**20, transcendentals=0
+        ),
+        name="experts_back" if backward else "experts",
+    )(*((packed, expert_in, expert_out) + ((kept,) if backward else ())))
 
 
 def slot_places(block_routes, experts, capacity):
@@ -80,6 +268,7 @@
     row_count, length = segments.shape
     seg_count = teacher.shape[1]
     capacity = max(2, 5 * tok_count // (2 * experts))
+    capacity = -(-capacity // 8) * 8
     allowed = key_allowed(segments, lengths)
     inputs = tokens.astype(jnp.float32).reshape(row_count, length, model_width)
     whole_weight = lax.all_gather(attn_weight, "expert", axis=1, tiled=True)
@@ -93,39 +282,30 @@
     normed_bf = normed_ffn.astype(jnp.bfloat16)
     slot_place = slot_places(routes, experts, capacity)
     slot_ids = jnp.arange(experts * capacity, dtype=jnp.int32)
-    dispatch = (slot_ids[:, None] == slot_place[None, :]).astype(jnp.bfloat16)
-    contract = (((1,), (1,)), ((), ()))
-
-    def spread_pairs(packed):
-        shaped = packed.reshape(experts, 1, capacity, model_width)
-        return jnp.broadcast_to(shaped, (experts, SPLIT, capacity, model_width)).reshape(
-            devices, capacity, model_width
+    places = slot_place.reshape(tok_count, 2)
+    chosen = [
+        (slot_ids[:, None] == places[None, :, choice]).astype(jnp.bfloat16) for choice in range(2)
+    ]
+
+    def fold_rows(packed):
+        shaped = packed.astype(jnp.bfloat16).reshape(experts, capacity, 2, model_width // 2)
+        return jnp.swapaxes(shaped, 1, 2).reshape(experts, 2 * capacity, model_width // 2)
+
+    def unfold_rows(returned):
+        shaped = returned.reshape(experts, 2, capacity, model_width // 2)
+        return jnp.swapaxes(shaped, 1, 2).reshape(experts * capacity, model_width)
+
+    def pick(rows, choice):
+        return lax.dot_general(
+            chosen[choice], rows, (((0,), (0,)), ((), ())), preferred_element_type=jnp.float32
         )
 
-    def join_halves(returned):
-        summed = jnp.sum(
-            returned.reshape(experts, SPLIT, capacity, model_width).astype(jnp.float32), axis=1
-        )
-        picked = jnp.take(summed.reshape(experts * capacity, model_width), slot_place, axis=0)
-        return picked.reshape(tok_count, 2, model_width)
-
-    rows_rep = jnp.repeat(normed_bf, 2, axis=0)
-    packed = jnp.dot(dispatch, rows_rep, preferred_element_type=jnp.float32).astype(jnp.bfloat16)
-    arrived = lax.all_to_all(
-        spread_pairs(packed), "expert", split_axis=0, concat_axis=0, tiled=True
-    )
-    pieces = arrived.shape[1]
-    flat_rows = arrived.reshape(devices * pieces, model_width)
-    activated = jnp.maximum(
-        jnp.dot(flat_rows, expert_in[0], preferred_element_type=jnp.float32), 0.0
-    ).astype(jnp.bfloat16)
-    partial_out = jnp.dot(activated, expert_out[0], preferred_element_type=jnp.float32).astype(
-        jnp.bfloat16
-    )
-    partial_out = partial_out.reshape(devices, pieces, model_width)
-    returned = lax.all_to_all(partial_out, "expert", split_axis=0, concat_axis=0, tiled=True)
-    returned, activated = (returned, activated.reshape(devices, pieces, activated.shape[1]))
-    expert_sum = jnp.sum(join_halves(returned) * route_gates[:, :, None], axis=1)
+    packed = jnp.dot(chosen[0] + chosen[1], normed_bf, preferred_element_type=jnp.float32)
+    returned, activated = run_experts(fold_rows(packed), expert_in, expert_out)
+    returned = unfold_rows(returned)
+    expert_sum = (
+        pick(returned, 0) * route_gates[:, 0:1] + pick(returned, 1) * route_gates[:, 1:2]
+    )
     outputs = hidden_flat + expert_sum
     positions = jnp.arange(length, dtype=jnp.int32)
     live_mask = positions[None, :] < lengths[:, None]
@@ -146,34 +326,23 @@
     grad_out = jnp.einsum(
         "rls,rsd->rld", member, difference, precision=lax.Precision.HIGHEST
     ).reshape(tok_count, model_width)
-    slot_grads = (
-        (grad_out[:, None, :] * route_gates[:, :, None])
-        .astype(jnp.bfloat16)
-        .reshape(2 * tok_count, model_width)
-    )
-    grad_packed = jnp.dot(dispatch, slot_grads, preferred_element_type=jnp.float32).astype(
-        jnp.bfloat16
-    )
-    grad_arrived = lax.all_to_all(
-        spread_pairs(grad_packed), "expert", split_axis=0, concat_axis=0, tiled=True
-    )
-    flat_grads = grad_arrived.reshape(devices * capacity, model_width)
-    act_flat = activated.reshape(devices * capacity, activated.shape[2])
-    product = lax.dot_general(
-        flat_grads, expert_out[0], contract, preferred_element_type=jnp.float32
-    )
-    grad_pre = jnp.where(act_flat > 0, product, 0.0).astype(jnp.bfloat16)
-    grad_part = lax.dot_general(
-        grad_pre, expert_in[0], contract, preferred_element_type=jnp.float32
-    ).astype(jnp.bfloat16)
-    grad_back = lax.all_to_all(
-        grad_part.reshape(devices, capacity, model_width),
-        "expert",
-        split_axis=0,
-        concat_axis=0,
-        tiled=True,
-    )
-    grad_normed = jnp.sum(join_halves(grad_back), axis=1)
+    slot_grads = jnp.concatenate(
+        [
+            (grad_out * route_gates[:, choice : choice + 1]).astype(jnp.bfloat16)
+            for choice in range(2)
+        ],
+        axis=0,
+    )
+    grad_packed = jnp.dot(
+        jnp.concatenate(chosen, axis=1), slot_grads, preferred_element_type=jnp.float32
+    )
+    grad_back = run_experts(fold_rows(grad_packed), expert_in, expert_out, activated)
+    grad_normed = lax.dot_general(
+        chosen[0] + chosen[1],
+        unfold_rows(grad_back),
+        (((0,), (0,)), ((), ())),
+        preferred_element_type=jnp.float32,
+    )
     grad_hidden = (grad_out + norm_pull(grad_normed)[0]).reshape(row_count, length, model_width)
     again_weight = lax.all_gather(attn_weight, "expert", axis=1, tiled=True)
 

time: 292 us -> 222 us (0.76)
  Pallas kernels: 0 us -> 87 us
  blocking collectives: 73.9 us -> 0 us
  waiting for transfers between devices: 132 us -> 73.2 us
  matrix products: 35.2 us -> 20.1 us
  starting transfers between devices: 9.36 us -> 0.04 us
  local copies, waits for them, and re-layouts: 9.75 us -> 16.2 us
  other arithmetic: 13.7 us -> 8.97 us
    pallas_call x0 -> x2, Pallas kernels: none -> 87 us  [run_experts(): pl.pallas_call(functools.partial(expert_kernel, chips, backward, groups_o...]
    all_to_all x2 -> x0, blocking collectives: 73.9 us -> none  [the longest x1 39.3 us: body(): lax.all_to_all(spread_pairs(grad_packed), 'expert', split_axis=0, concat_...]
    all_to_all x2 -> x0, waiting for transfers between devices: 54 us -> none  [the longest x1 27.2 us: body(): lax.all_to_all(grad_part.reshape(devices, capacity, model_width), 'expert...]
    dot_general x5, matrix products: 18.7 us -> 2.81 us  [the longest x1 1.25 us: body(): jnp.dot(jnp.concatenate(chosen, axis=1), slot_grads, preferred_element_ty...]
    all_to_all x2 -> x0, starting transfers between devices: 9.32 us -> none  [the longest x1 4.7 us: body(): lax.all_to_all(partial_out, 'expert', split_axis=0, concat_axis=0, tiled=...]
    reduce_sum x5 -> x0, other arithmetic: 6.23 us -> none  [the longest x2 3.44 us: join_halves(): jnp.sum(returned.reshape(experts, SPLIT, capacity, model_width).astype(jn...]
    unnamed x40 -> x97, local copies, waits for them, and re-layouts: 2.51 us -> 8.11 us
    all_gather x1, waiting for transfers between devices: 77.3 us -> 72.5 us  [body(): whole_weight = lax.all_gather(attn_weight, 'expert', axis=1, tiled=True)]
  transfers between devices with their start and end apart: 3 -> 1, of which waited for: 3 -> 1; matrix products, arithmetic and copies ran while one was open for 2% -> 4% of each run, Pallas kernels for 0% -> 0%
where the time goes in v1:
time: 222 us; the launch traced here: 221 us
  Pallas kernels  87 us (39%)
  waiting for transfers between devices  73.2 us (33%)
  matrix products  20.1 us (9%)
  local copies, waits for them, and re-layouts  16.2 us (7%)
  between operations  15.5 us (7%)
  other arithmetic  8.97 us (4%)
    pallas_call x2, Pallas kernels, run_experts(): pl.pallas_call(functools.partial(expert_kernel, chips, backward, groups_o...  87 us
    all_gather x1, waiting for transfers between devices, body(): whole_weight = lax.all_gather(attn_weight, 'expert', axis=1, tiled=True)  72.5 us
    dot_general x2, matrix products, attend(): jnp.dot(normed, weight[:, :3 * model_width], preferred_element_type=jnp.f...  9.12 us
    unnamed x97, local copies, waits for them, and re-layouts  8.11 us
    reshape x4, local copies, waits for them, and re-layouts, fold_rows(): packed.astype(jnp.bfloat16).reshape(experts, capacity, 2, model_width // 2)  4.68 us
    dot_general x2, matrix products, attend(): jnp.dot(context, weight[:, 3 * model_width:], preferred_element_type=jnp....  4.56 us
  transfers between devices with their start and end apart: 1, of which 1 were waited for; matrix products, arithmetic and copies ran while one was open for 4% of the time, Pallas kernels for 0%

profile of v1, /device:TPU:0, one launch (start us, length us, event | category | flops | bytes accessed | tf_op | source)
XLA Modules:
  0.0 221.0 jit_solution(16466332018249005597)
XLA Ops:
  7.2 0.7 all-gather.2.cloned.1.call-update
  7.9 0.8 copy.87
  9.6 0.6 reduce-window.6
  10.8 0.8 convert_reduce_fusion.1
  11.6 1.1 convert_reduce_fusion
  12.7 1.2 fusion.41
  13.9 0.6 copy-done.40
  14.4 0.6 maximum_convert_fusion
  15.0 0.7 multiply_add_fusion
  15.7 1.3 slice_bitcast_fusion
  17.0 0.8 fusion.65
  17.8 0.7 fusion.60
  18.5 72.5 %all-gather.2.cloned.1.call-done = bf16[1024,4096]{1,0:T(8,128)(2,1)} async-done(((bf16[1024,256]{1,0:T(8,128)(2,1)}), bf16[1024,4096]{1,0:T(8,128)(2,1)}) %all-gather.2.cloned.1.call-update) | async-done | bytes 8388624 | tf_op jit(solution)/shard_map/all_gather | solution.py:274
  91.0 4.0 %fusion.11 = bf16[16,8,24,128]{3,1,2,0:T(8,128)(2,1)S(1)} fusion(bf16[1024,4096]{1,0:T(8,128)(2,1)} %all-gather.2.cloned.1.call-done, bf16[128,1024]{1,0:T(8,128)(2,1)} %param.11, f32[1024]{0:T(1024)} %param.14, f32[128]{0:T(128)S(1)} %fusion.91, f32[128]{0:T(128)S(1)} %broadcast_multiply_fusion.1), kind=kOutput, calls=%fused_computation.11 | convolution fusion | flops 806354944 | bytes 7345152 | tf_op jit(solution)/shard_map/dot_general | solution.py:41
  96.0 0.7 multiply_divide_fusion
  96.9 2.1 fusion.97
  99.9 0.5 copy-done.36
  100.8 0.5 reshape.546
  101.4 2.2 copy-done
  103.6 44.0 %experts.1 = (bf16[8,80,512]{2,1,0:T(8,128)(2,1)S(1)}, bf16[640,2048]{1,0:T(8,128)(2,1)S(1)}) custom-call(bf16[8,80,512]{2,1,0:T(8,128)(2,1)S(1)} %bitcast.107, bf16[1,1024,2048]{2,1,0:T(8,128)(2,1)S(1)} %copy-done, bf16[1,2048,1024]{2,1,0:T(8,128)(2,1)} %refs_2_.3), custom_call_target="tpu_custom_call" | custom-call | flops 5368709120 | bytes 20971520 | tf_op jit(solution)/shard_map/experts/pallas_call | solution.py:213
  147.6 0.5 copy.91
  149.4 0.6 copy-done.14
  150.1 1.5 multiply_convert_fusion.1
  151.5 1.3 convolution_convert_fusion.1
  152.8 3.0 %reshape.551 = bf16[8,40,2,512]{3,2,1,0:T(2,128)(2,1)} reshape(bf16[320,1024]{1,0:T(8,128)(2,1)} %convolution_convert_fusion.1) | data formatting | bytes 1310720 | tf_op jit(solution)/shard_map/reshape | solution.py:291
  155.8 1.2 copy.92
  156.9 2.2 copy-done.1
  159.2 43.0 %experts_back.1 = bf16[8,80,512]{2,1,0:T(8,128)(2,1)S(1)} custom-call(bf16[8,80,512]{2,1,0:T(8,128)(2,1)S(1)} %bitcast.109, bf16[1,1024,2048]{2,1,0:T(8,128)(2,1)S(1)} %copy-done.1, bf16[1,2048,1024]{2,1,0:T(8,128)(2,1)} %refs_2_.3, bf16[640,2048]{1,0:T(8,128)(2,1)S(1)} %get-tuple-element.5.refs_3_), custom_call_target="tpu_custom_call" | custom-call | flops 5368709120 | bytes 20971520 | tf_op jit(solution)/shard_map/experts_back/pallas_call | solution.py:213
  202.2 0.5 copy.93
  203.7 2.4 %fusion.20 = bf16[128,1024]{1,0:T(8,128)(2,1)S(1)} fusion(bf16[1024,4096]{1,0:T(8,128)(2,1)} %all-gather.2.cloned.1.call-done, f32[128,1024]{1,0:T(8,128)S(1)} %copy-done.3, f32[128,1024]{1,0:T(8,128)S(1)} %get-tuple-element.7, f32[128]{0:T(128)S(1)} %negate_multiply_fusion.1), kind=kOutput, calls=%fused_computation.20 | convolution fusion | flops 268828672 | bytes 3408384 | tf_op jit(solution)/shard_map/transpose(jvp())/dot_general | solution.py:59
  207.8 5.1 %fusion.44 = (f32[128]{0:T(128)S(1)}, f32[128,1024]{1,0:T(8,128)S(1)}) fusion(bf16[128,1024]{1,0:T(8,128)(2,1)S(1)} %copy-done.2, f32[128]{0:T(128)S(1)} %copy-done.32, f32[1024]{0:T(1024)S(1)} %copy-done.45, bf16[128,3072]{0,1:T(8,128)(2,1)S(1)} %bitcast.119, bf16[1024,4096]{1,0:T(8,128)(2,1)} %all-gather.2.cloned.1.call-done), kind=kOutput, calls=%fused_computation.47 | convolution fusion | flops 806223744 | bytes 7869440 | tf_op jit(solution)/shard_map/transpose(jvp())/dot_general | solution.py:41
  213.2 1.0 add_convert_fusion
  (130 shorter events, 7.1 us)
Async XLA Ops:
  7.2 83.8 %all-gather.2.cloned.1.call-start = ((), (), s32[]{:S(2)}) async-start(), calls=%async_computation | async-start | bytes 8912896 | tf_op jit(solution)/shard_map/all_gather | solution.py:274
  10.8 84.5 %copy-start.28 = (pred[128]{0:T(512)(128)(4,1)}, pred[128]{0:T(512)(128)(4,1)S(1)}, u32[]{:S(2)}) copy-start(pred[128]{0:T(512)(128)(4,1)S(1)} %iota_compare_fusion.10) | copy-start | bytes 388
  12.7 82.7 %copy-start.31 = (f32[128]{0:T(128)}, f32[128]{0:T(128)S(1)}, u32[]{:S(2)}) copy-start(f32[128]{0:T(128)S(1)} %broadcast_multiply_fusion.1) | copy-start | bytes 1540
  14.4 81.2 %copy-start.38 = (f32[128]{0:T(128)}, f32[128]{0:T(128)S(1)}, u32[]{:S(2)}) copy-start(f32[128]{0:T(128)S(1)} %fusion.91) | copy-start | bytes 1540
  15.7 83.6 %copy-start.19 = (s32[128]{0:T(128)}, s32[128]{0:T(128)S(1)}, u32[]{:S(2)}) copy-start(s32[128]{0:T(128)S(1)} %get-tuple-element.16) | copy-start | bytes 1540
  15.7 83.6 %copy-start.22 = (s32[128]{0:T(128)}, s32[128]{0:T(128)S(1)}, u32[]{:S(2)}) copy-start(s32[128]{0:T(128)S(1)} %get-tuple-element.15) | copy-start | bytes 1540
  18.5 78.4 %copy-start.2 = (bf16[128,1024]{1,0:T(8,128)(2,1)S(1)}, bf16[128,1024]{1,0:T(8,128)(2,1)}, u32[]{:S(2)}) copy-start(bf16[128,1024]{1,0:T(8,128)(2,1)} %param.11) | copy-start | bytes 786436
  95.0 5.4 %copy-start.16 = (f32[1024]{0:T(1024)S(1)}, f32[1024]{0:T(1024)}, u32[]{:S(2)}) copy-start(f32[1024]{0:T(1024)} %param.16) | copy-start | bytes 12292
  95.3 4.0 %copy-start.9 = (bf16[1,128,1,8,128]{4,3,2,1,0:T(8,128)(2,1)}, bf16[1,128,1,8,128]{4,3,2,1,0:T(8,128)(2,1)S(1)}, u32[]{:S(2)}) copy-start(bf16[1,128,1,8,128]{4,3,2,1,0:T(8,128)(2,1)S(1)} %get-tuple-element.9) | copy-start | bytes 786436
  95.3 4.0 %copy-start.11 = (bf16[1,128,1,8,128]{4,3,2,1,0:T(8,128)(2,1)}, bf16[1,128,1,8,128]{4,3,2,1,0:T(8,128)(2,1)S(1)}, u32[]{:S(2)}) copy-start(bf16[1,128,1,8,128]{4,3,2,1,0:T(8,128)(2,1)S(1)} %get-tuple-element.10) | copy-start | bytes 786436
  103.6 44.7 %copy-start.20 = (s32[128]{0:T(128)S(1)}, s32[128]{0:T(128)}, u32[]{:S(2)}) copy-start(s32[128]{0:T(128)} %copy-done.19) | copy-start | bytes 1540
  103.6 44.7 %copy-start.30 = (f32[128]{0:T(128)S(1)}, f32[128]{0:T(128)}, u32[]{:S(2)}) copy-start(f32[128]{0:T(128)} %get-tuple-element.14) | copy-start | bytes 1540
  103.6 45.1 %copy-start.23 = (s32[128]{0:T(128)S(1)}, s32[128]{0:T(128)}, u32[]{:S(2)}) copy-start(s32[128]{0:T(128)} %copy-done.22) | copy-start | bytes 1540
  103.6 45.1 %copy-start.33 = (f32[128]{0:T(128)S(1)}, f32[128]{0:T(128)}, u32[]{:S(2)}) copy-start(f32[128]{0:T(128)} %get-tuple-element.13) | copy-start | bytes 1540
  103.6 45.5 %copy-start.25 = (s32[1,128]{1,0:T(1,128)S(1)}, s32[1,128]{1,0:T(1,128)}, u32[]{:S(2)}) copy-start(s32[1,128]{1,0:T(1,128)} %param.12) | copy-start | bytes 1540
  103.6 45.5 %copy-start.29 = (pred[128]{0:T(512)(128)(4,1)S(1)}, pred[128]{0:T(512)(128)(4,1)}, u32[]{:S(2)}) copy-start(pred[128]{0:T(512)(128)(4,1)} %copy-done.28) | copy-start | bytes 388
  103.6 45.5 %copy-start.42 = (f32[4]{0:T(128)S(1)}, f32[4]{0:T(128)}, u32[]{:S(2)}) copy-start(f32[4]{0:T(128)} %maximum_convert_fusion) | copy-start | bytes 52
  159.1 43.8 %copy-start.17 = (f32[1024]{0:T(1024)S(1)}, f32[1024]{0:T(1024)}, u32[]{:S(2)}) copy-start(f32[1024]{0:T(1024)} %param.16) | copy-start | bytes 12292
  159.1 43.8 %copy-start.21 = (s32[128]{0:T(128)S(1)}, s32[128]{0:T(128)}, u32[]{:S(2)}) copy-start(s32[128]{0:T(128)} %copy-done.19) | copy-start | bytes 1540
  159.1 43.8 %copy-start.24 = (s32[128]{0:T(128)S(1)}, s32[128]{0:T(128)}, u32[]{:S(2)}) copy-start(s32[128]{0:T(128)} %copy-done.22) | copy-start | bytes 1540
  159.1 43.8 %copy-start.27 = (f32[128]{0:T(128)S(1)}, f32[128]{0:T(128)}, u32[]{:S(2)}) copy-start(f32[128]{0:T(128)} %copy-done.26) | copy-start | bytes 1540
  159.1 44.2 %copy-start.44 = (f32[128]{0:T(128)S(1)}, f32[128]{0:T(128)}, u32[]{:S(2)}) copy-start(f32[128]{0:T(128)} %copy-done.43) | copy-start | bytes 1540
  159.2 44.3 %copy-start.37 = (f32[128]{0:T(128)S(1)}, f32[128]{0:T(128)}, u32[]{:S(2)}) copy-start(f32[128]{0:T(128)} %copy-done.36) | copy-start | bytes 1540
  159.2 44.5 %copy-start.3 = (f32[128,1024]{1,0:T(8,128)S(1)}, f32[128,1024]{1,0:T(8,128)}, u32[]{:S(2)}) copy-start(f32[128,1024]{1,0:T(8,128)} %get-tuple-element.21) | copy-start | bytes 1572868
  202.2 4.1 %copy-start.8 = (f32[8,128,128]{1,2,0:T(8,128)S(1)}, f32[8,128,128]{1,2,0:T(8,128)}, u32[]{:S(2)}) copy-start(f32[8,128,128]{1,2,0:T(8,128)} %copy-done.7) | copy-start | bytes 1572868
  202.2 4.1 %copy-start.35 = (f32[8,128]{1,0:T(8,128)S(1)}, f32[8,128]{1,0:T(8,128)}, u32[]{:S(2)}) copy-start(f32[8,128]{1,0:T(8,128)} %copy-done.34) | copy-start | bytes 12292
  202.2 4.4 %copy-start.6 = (bf16[1,128,1,8,128]{1,4,3,2,0:T(8,128)(2,1)S(1)}, bf16[1,128,1,8,128]{1,4,3,2,0:T(8,128)(2,1)}, u32[]{:S(2)}) copy-start(bf16[1,128,1,8,128]{1,4,3,2,0:T(8,128)(2,1)} %copy-done.5) | copy-start | bytes 786436
  202.2 4.4 %copy-start.18 = (f32[8,128]{1,0:T(8,128)S(1)}, f32[8,128]{1,0:T(8,128)}, u32[]{:S(2)}) copy-start(f32[8,128]{1,0:T(8,128)} %multiply_divide_fusion) | copy-start | bytes 12292
  202.8 4.2 %copy-start.12 = (bf16[1,128,1,8,128]{4,3,2,1,0:T(8,128)(2,1)S(1)}, bf16[1,128,1,8,128]{4,3,2,1,0:T(8,128)(2,1)}, u32[]{:S(2)}) copy-start(bf16[1,128,1,8,128]{4,3,2,1,0:T(8,128)(2,1)} %copy-done.11) | copy-start | bytes 786436
  207.6 5.3 %copy-start.41 = (f32[128]{0:T(128)S(1)}, f32[128]{0:T(128)}, u32[]{:S(2)}) copy-start(f32[128]{0:T(128)} %copy-done.40) | copy-start | bytes 1540
  207.6 5.3 %copy-start.39 = (f32[128]{0:T(128)S(1)}, f32[128]{0:T(128)}, u32[]{:S(2)}) copy-start(f32[128]{0:T(128)} %copy-done.38) | copy-start | bytes 1540
  207.7 5.6 %copy-start.4 = (f32[128,1024]{1,0:T(8,128)S(1)}, f32[128,1024]{1,0:T(8,128)}, u32[]{:S(2)}) copy-start(f32[128,1024]{1,0:T(8,128)} %get-tuple-element.21) | copy-start | bytes 1572868
  (15 other events, 23.9 us)
Sparse Core Ops, SparseCore 0:
  10.2 80.8 all-gather.1

commit v2 on v1

--- a/solution.py
+++ b/solution.py
@@ -38,8 +38,8 @@
     normed = (
         layer_norm(inputs, scale_gain).astype(jnp.bfloat16).reshape(row_count * length, model_width)
     )
-    projected = jnp.dot(
-        normed, weight[:, : 3 * model_width], preferred_element_type=jnp.float32
+    projected = lax.dot_general(
+        normed, weight[: 3 * model_width], NT, preferred_element_type=jnp.float32
     ).astype(jnp.bfloat16)
     projected = projected.reshape(row_count, length, 3, head_count, head_width)
     queries = projected[:, :, 0]
@@ -56,7 +56,7 @@
         "rhqk,rkhd->rqhd", probabilities, values_all, preferred_element_type=jnp.float32
     ).astype(jnp.bfloat16)
     context = context.reshape(row_count * length, model_width)
-    output = jnp.dot(context, weight[:, 3 * model_width :], preferred_element_type=jnp.float32)
+    output = lax.dot_general(context, weight[3 * model_width :], NT, preferred_element_type=jnp.float32)
     return inputs + output.reshape(row_count, length, model_width)
 
 
@@ -84,12 +84,12 @@
 
 def expert_kernel(chips, backward, groups_of, *refs):
     if backward:
-        packed, w1_hbm, w2_hbm, kept, out = refs[:5]
+        rows_in, w1_hbm, w2_hbm, kept, rows_out = refs[:5]
         rest = refs[5:]
     else:
-        packed, w1_hbm, w2_hbm, out, kept = refs[:5]
+        rows_in, w1_hbm, w2_hbm, rows_out, kept = refs[:5]
         rest = refs[5:]
-    (w1, w2, got_a, got_b, x_ref, h_scr, part, to_pair, from_pair, to_back,
+    (packed, out, w1, w2, got_a, got_b, x_ref, h_scr, part, to_pair, from_pair, to_back,
      w_sem, send_a, recv_a, send_b, recv_b, send_c, recv_c, send_d, recv_d) = rest
     rank = lax.axis_index("expert")
     core = lax.rem(rank, 2)
@@ -100,6 +100,8 @@
     load_2 = pltpu.make_async_copy(w2_hbm.at[0], w2, w_sem.at[1])
     load_1.start()
     load_2.start()
+    for e in range(chips):
+        packed[e] = fold(rows_in[pl.ds(e * cap, cap), :]).astype(jnp.bfloat16)
     peer_chip = [flip(chip, k, chips) for k in range(chips)]
     peer = [2 * peer_chip[k] + core for k in range(chips)]
     barrier = pltpu.get_barrier_semaphore()
@@ -196,19 +198,141 @@
             back[k].wait_recv()
         across[k].wait_send()
         over[k].wait_send()
-
-
-def run_experts(packed, expert_in, expert_out, kept=None):
-    chips, rows2, half = packed.shape
+    for e in range(chips):
+        rows_out[pl.ds(e * cap, cap), :] = unfold(out[e])
+
+
+def gather_kernel(devices, own, out, local_sem, send, recv):
+    lines = devices // 4
+    width = own.shape[1]
+    half, quarter = width // 2, width // 4
+    rank = lax.axis_index("expert")
+    group = lax.axis_index("groups")
+    core = lax.rem(rank, 2)
+    side = lax.rem(lax.div(rank, 2), 2)
+    line = lax.div(rank, 4)
+    there = [flip(line, k, lines) for k in range(lines)]
+
+    def name(k, x, c):
+        return there[k] * 4 + x * 2 + c
+
+    pair = {"expert": name(0, side, 1 - core)}
+    x_peer = {"expert": name(0, 1 - side, core)}
+    y_peer = {"groups": 1 - group, "expert": rank}
+    z_peer = [{"expert": name(k, side, core)} for k in range(lines)]
+    barrier = pltpu.get_barrier_semaphore()
+    for target in [pair, x_peer, y_peer] + z_peer[1:]:
+        pl.semaphore_signal(barrier, inc=1, device_id=target, device_id_type=MESH)
+    pl.semaphore_wait(barrier, lines + 2)
+
+    mine = (group * half, half)
+    other = ((1 - group) * half, half)
+    started = []
+
+    def copy(kind, k, target, shard, columns, source=None):
+        place = pl.ds(pl.multiple_of(columns[0], quarter), columns[1])
+        dst = out.at[shard, :, place]
+        src = dst if source is None else source.at[:, place]
+        return pltpu.make_async_remote_copy(
+            src_ref=src, dst_ref=dst, send_sem=send.at[kind, k], recv_sem=recv.at[kind, k],
+            device_id=target, device_id_type=MESH,
+        )
+
+    def go(*args):
+        made = copy(*args)
+        made.start()
+        started.append(made)
+
+    ahead = side, core
+    keep = pltpu.make_async_copy(own, out.at[rank], local_sem)
+    keep.start()
+    go(1, 0, x_peer, rank, mine, own)
+    for k in range(1, lines):
+        go(0, k, z_peer[k], rank, mine, own)
+    go(4, 0, x_peer, rank, (other[0] + quarter, quarter), own)
+    go(5, 0, pair, rank, (0, width), own)
+
+    def landed(kind, k, shard, columns):
+        copy(kind, k, pair, shard, columns).wait_recv()
+
+    def first(k):
+        shard = name(k, *ahead)
+        landed(0, k, shard, mine)
+        go(1, k, x_peer, shard, mine)
+        go(2, k, y_peer, shard, mine)
+        go(5, k, pair, shard, mine)
+
+    def second(k):
+        if k:
+            shard = name(k, *ahead)
+            landed(2, k, shard, other)
+            go(4, k, x_peer, shard, (other[0] + quarter, quarter))
+            go(7, k, pair, shard, other)
+        shard = name(k, 1 - side, core)
+        landed(1, k, shard, mine)
+        go(3, k, y_peer, shard, (mine[0], quarter))
+        go(6, k, pair, shard, mine)
+
+    def third(k):
+        shard = name(k, 1 - side, core)
+        landed(4, k, shard, (other[0] + quarter, quarter))
+        go(9, k, pair, shard, (other[0] + quarter, quarter))
+        landed(3, k, shard, (other[0], quarter))
+        go(8, k, pair, shard, (other[0], quarter))
+
+    second(0)
+    for k in range(1, lines):
+        first(k)
+        if k > 1:
+            second(k - 1)
+        third(k - 1)
+    second(lines - 1)
+    third(lines - 1)
+
+    for k in range(lines):
+        shard = name(k, side, 1 - core)
+        across = name(k, 1 - side, 1 - core)
+        if k:
+            landed(5, k, shard, mine)
+            landed(7, k, shard, other)
+        else:
+            landed(5, 0, shard, (0, width))
+        landed(6, k, across, mine)
+        landed(8, k, across, (other[0], quarter))
+        landed(9, k, across, (other[0] + quarter, quarter))
+    for made in started:
+        made.wait_send()
+    keep.wait()
+
+
+def gather_weight(own, devices):
+    lines = devices // 4
+    gathered = pl.pallas_call(
+        functools.partial(gather_kernel, devices),
+        out_shape=jax.ShapeDtypeStruct((devices,) + own.shape, own.dtype),
+        in_specs=[pl.BlockSpec(memory_space=pltpu.HBM)],
+        out_specs=pl.BlockSpec(memory_space=pltpu.HBM),
+        scratch_shapes=[
+            pltpu.SemaphoreType.DMA,
+            pltpu.SemaphoreType.DMA((10, lines)),
+            pltpu.SemaphoreType.DMA((10, lines)),
+        ],
+        compiler_params=pltpu.CompilerParams(collective_id=2, has_side_effects=True),
+        name="gather_weight",
+    )(own)
+    return gathered.reshape(devices * own.shape[0], own.shape[1])
+
+
+def run_experts(rows_in, chips, expert_in, expert_out, kept=None):
     backward = kept is not None
-    rows = chips * rows2
+    rows = 2 * rows_in.shape[0]
     width, hidden = expert_in.shape[1:]
     groups_of = [list(range(chips // 2)), list(range(chips // 2, chips))]
     vmem = pl.BlockSpec(memory_space=pltpu.VMEM)
-    hbm = pl.BlockSpec(memory_space=pl.ANY)
-    message = jax.ShapeDtypeStruct(packed.shape, jnp.bfloat16)
+    hbm = pl.BlockSpec(memory_space=pltpu.HBM)
+    message = jax.ShapeDtypeStruct(rows_in.shape, jnp.float32)
     kept_shape = jax.ShapeDtypeStruct((rows, hidden), jnp.bfloat16)
-    block = pltpu.VMEM(packed.shape, jnp.bfloat16)
+    block = pltpu.VMEM((chips, rows // chips, width // 2), jnp.bfloat16)
     sems = pltpu.SemaphoreType.DMA((chips,))
     return pl.pallas_call(
         functools.partial(expert_kernel, chips, backward, groups_of),
@@ -216,6 +340,8 @@
         in_specs=[vmem, hbm, hbm] + ([vmem] if backward else []),
         out_specs=vmem if backward else (vmem, vmem),
         scratch_shapes=[
+            block,
+            block,
             pltpu.VMEM((width, hidden), jnp.bfloat16),
             pltpu.VMEM((hidden, width), jnp.bfloat16),
             block,
@@ -238,7 +364,7 @@
             flops=4 * rows * width * hidden, bytes_accessed=20 * 2**20, transcendentals=0
         ),
         name="experts_back" if backward else "experts",
-    )(*((packed, expert_in, expert_out) + ((kept,) if backward else ())))
+    )(*((rows_in, expert_in, expert_out) + ((kept,) if backward else ())))
 
 
 def slot_places(block_routes, experts, capacity):
@@ -271,7 +397,7 @@
     capacity = -(-capacity // 8) * 8
     allowed = key_allowed(segments, lengths)
     inputs = tokens.astype(jnp.float32).reshape(row_count, length, model_width)
-    whole_weight = lax.all_gather(attn_weight, "expert", axis=1, tiled=True)
+    whole_weight = gather_weight(attn_weight.T, devices)
     hidden_state = attend(inputs, whole_weight, allowed, attn_gain, HEADS)
     hidden_flat = hidden_state.reshape(tok_count, model_width)
 
@@ -287,22 +413,14 @@
         (slot_ids[:, None] == places[None, :, choice]).astype(jnp.bfloat16) for choice in range(2)
     ]
 
-    def fold_rows(packed):
-        shaped = packed.astype(jnp.bfloat16).reshape(experts, capacity, 2, model_width // 2)
-        return jnp.swapaxes(shaped, 1, 2).reshape(experts, 2 * capacity, model_width // 2)
-
-    def unfold_rows(returned):
-        shaped = returned.reshape(experts, 2, capacity, model_width // 2)
-        return jnp.swapaxes(shaped, 1, 2).reshape(experts * capacity, model_width)
-
     def pick(rows, choice):
         return lax.dot_general(
             chosen[choice], rows, (((0,), (0,)), ((), ())), preferred_element_type=jnp.float32
         )
 
     packed = jnp.dot(chosen[0] + chosen[1], normed_bf, preferred_element_type=jnp.float32)
-    returned, activated = run_experts(fold_rows(packed), expert_in, expert_out)
-    returned = unfold_rows(returned)
+    returned, activated = run_experts(packed, experts, expert_in, expert_out)
+    returned = returned.astype(jnp.bfloat16)
     expert_sum = (
         pick(returned, 0) * route_gates[:, 0:1] + pick(returned, 1) * route_gates[:, 1:2]
     )
@@ -336,18 +454,17 @@
     grad_packed = jnp.dot(
         jnp.concatenate(chosen, axis=1), slot_grads, preferred_element_type=jnp.float32
     )
-    grad_back = run_experts(fold_rows(grad_packed), expert_in, expert_out, activated)
+    grad_back = run_experts(grad_packed, experts, expert_in, expert_out, activated)
     grad_normed = lax.dot_general(
         chosen[0] + chosen[1],
-        unfold_rows(grad_back),
+        grad_back.astype(jnp.bfloat16),
         (((0,), (0,)), ((), ())),
         preferred_element_type=jnp.float32,
     )
     grad_hidden = (grad_out + norm_pull(grad_normed)[0]).reshape(row_count, length, model_width)
-    again_weight = lax.all_gather(attn_weight, "expert", axis=1, tiled=True)
 
     def attention_again(source):
-        return attend(source, again_weight, allowed, attn_gain, HEADS)
+        return attend(source, whole_weight, allowed, attn_gain, HEADS)
 
     grad_inputs = jax.vjp(attention_again, inputs)[1](grad_hidden)[0]
     grad_tokens = grad_inputs.reshape(tok_count, model_width).astype(jnp.bfloat16)

time: 222 us -> 176 us (0.79)
  waiting for transfers between devices: 73.2 us -> 0 us
  Pallas kernels: 87 us -> 138 us
  between operations: 15.5 us -> 1.7 us
  matrix products: 20.1 us -> 12.4 us
    all_gather x1 -> x0, waiting for transfers between devices: 72.5 us -> none  [body(): whole_weight = lax.all_gather(attn_weight, 'expert', axis=1, tiled=True)]
    pallas_call x0 -> x1, Pallas kernels: none -> 50.1 us  [gather_weight(): pl.pallas_call(functools.partial(gather_kernel, devices), out_shape=jax.S...]
    dot_general x5, matrix products: 14.1 us -> 5.85 us  [the longest x2 3.35 us: attend(): lax.dot_general(normed, weight[:3 * model_width], NT, preferred_element_t...]
    slice x1 -> x3, local copies, waits for them, and re-layouts: 0.21 us -> 6.24 us  [the longest x1 4.26 us: attend(): weight[:3 * model_width]]
    reshape x6 -> x0, local copies, waits for them, and re-layouts: 5.77 us -> none  [the longest x4 4.68 us: fold_rows(): packed.astype(jnp.bfloat16).reshape(experts, capacity, 2, model_width // 2)]
    unnamed x97 -> x44, local copies, waits for them, and re-layouts: 8.11 us -> 6.9 us
  transfers between devices with their start and end apart: 1 -> 0, of which waited for: 1 -> 0; matrix products, arithmetic and copies ran while one was open for 4% -> 0% of each run, Pallas kernels for 0% -> 0%
where the time goes in v2:
time: 176 us
  Pallas kernels  138 us (78%)
  local copies, waits for them, and re-layouts  17 us (10%)
  matrix products  12.4 us (7%)
  other arithmetic  7.18 us (4%)
    pallas_call x2, Pallas kernels, run_experts(): pl.pallas_call(functools.partial(expert_kernel, chips, backward, groups_o...  87.5 us
    pallas_call x1, Pallas kernels, gather_weight(): pl.pallas_call(functools.partial(gather_kernel, devices), out_shape=jax.S...  50.1 us
    unnamed x44, local copies, waits for them, and re-layouts  6.9 us
    slice x1, local copies, waits for them, and re-layouts, attend(): weight[:3 * model_width]  4.26 us

profile of v2, /device:TPU:0, one launch (start us, length us, event | category | flops | bytes accessed | tf_op | source)
XLA Modules:
  0.0 175.9 jit_solution(2488060687216539111)
XLA Ops:
  1.3 0.8 convert_reduce_fusion.1
  2.1 1.1 convert_reduce_fusion
  3.1 1.2 fusion.16
  4.3 0.8 slice_bitcast_fusion
  5.1 0.8 fusion.44
  5.9 0.8 copy.78
  7.0 0.6 reduce-window.6
  8.2 0.7 multiply_add_fusion
  8.9 2.1 %copy.73 = bf16[1024,256]{0,1:T(8,128)(2,1)} copy(bf16[1024,256]{1,0:T(8,128)(2,1)} %param.15) | data formatting | bytes 1048576 | tf_op args[4]
  11.0 50.1 %gather_weight.1 = bf16[16,256,1024]{2,1,0:T(8,128)(2,1)} custom-call(bf16[256,1024]{1,0:T(8,128)(2,1)} %bitcast.103), custom_call_target="tpu_custom_call" | custom-call | tf_op jit(solution)/shard_map/gather_weight/pallas_call | solution.py:310
  61.1 1.8 %slice.51 = bf16[4,256,1024]{2,1,0:T(8,128)(2,1)S(1)} slice(bf16[16,256,1024]{2,1,0:T(8,128)(2,1)} %gather_weight.1), slice={[12:16], [0:256], [0:1024]} | slice | bytes 4194304 | tf_op jit(solution)/shard_map/slice | solution.py:59
  62.9 4.3 %slice.46 = bf16[12,256,1024]{2,1,0:T(8,128)(2,1)S(1)} slice(bf16[16,256,1024]{2,1,0:T(8,128)(2,1)} %gather_weight.1), slice={[0:12], [0:256], [0:1024]} | slice | bytes 12582912 | tf_op jit(solution)/shard_map/slice | solution.py:42
  67.2 2.2 %fusion = bf16[16,8,24,128]{3,1,2,0:T(8,128)(2,1)S(1)} fusion(bf16[3072,1024]{1,0:T(8,128)(2,1)S(1)} %bitcast.95, bf16[128,1024]{1,0:T(8,128)(2,1)S(1)} %copy-done.4, f32[1024]{0:T(1024)S(1)} %copy-done.14, f32[128]{0:T(128)S(1)} %fusion.70, f32[128]{0:T(128)S(1)} %broadcast_multiply_fusion.1), kind=kOutput, calls=%fused_computation.1 | convolution fusion | flops 806354944 | bytes 7345152 | tf_op jit(solution)/shard_map/dot_general | solution.py:41
  69.5 0.4 copy-done.1
  70.0 0.8 fusion.75
  71.1 1.4 multiply_reduce_fusion.3
  72.8 0.5 copy-done.8
  73.3 0.9 fusion.76
  74.5 0.4 fusion.26.refs_0_
  74.9 0.6 copy-done
  75.5 43.9 %experts.1 = (f32[320,1024]{1,0:T(8,128)S(1)}, bf16[640,2048]{1,0:T(8,128)(2,1)S(1)}) custom-call(f32[320,1024]{1,0:T(8,128)S(1)} %fusion.26.refs_0_, bf16[1,1024,2048]{2,1,0:T(8,128)(2,1)S(1)} %copy-done, bf16[1,2048,1024]{2,1,0:T(8,128)(2,1)} %refs_2_.3), custom_call_target="tpu_custom_call" | custom-call | flops 5368709120 | bytes 20971520 | tf_op jit(solution)/shard_map/experts/pallas_call | solution.py:337
  120.2 0.4 fusion.10
  120.6 0.6 multiply_convert_fusion.1
  121.6 43.5 %experts_back.1 = f32[320,1024]{1,0:T(8,128)S(1)} custom-call(f32[320,1024]{1,0:T(8,128)S(1)} %fusion.20.refs_0_, bf16[1,1024,2048]{2,1,0:T(8,128)(2,1)S(1)} %copy-done, bf16[1,2048,1024]{2,1,0:T(8,128)(2,1)} %refs_2_.3, bf16[640,2048]{1,0:T(8,128)(2,1)S(1)} %get-tuple-element.5.refs_3_), custom_call_target="tpu_custom_call" | custom-call | flops 5368709120 | bytes 20971520 | tf_op jit(solution)/shard_map/experts_back/pallas_call | solution.py:337
  165.1 0.4 multiply_reduce_fusion.1
  165.9 0.9 copy-done.3
  166.7 1.2 convolution_convert_fusion.6
  167.9 1.8 %copy.95 = bf16[128,1024]{0,1:T(8,128)(2,1)} copy(bf16[128,1024]{1,0:T(8,128)(2,1)} %convolution_convert_fusion.6) | data formatting | bytes 524288 | tf_op jit(solution)/shard_map/transpose(jvp())/reshape | solution.py:58
  169.7 1.5 fusion.7
  172.3 1.1 slice-done.1
  173.5 1.1 fusion.19
  174.9 1.0 add_convert_fusion
  (72 shorter events, 4.4 us)
Async XLA Ops:
  62.9 10.4 %copy-start.2 = (bf16[4,256,1024]{2,1,0:T(8,128)(2,1)}, bf16[4,256,1024]{2,1,0:T(8,128)(2,1)S(1)}, u32[]{:S(2)}) copy-start(bf16[4,256,1024]{2,1,0:T(8,128)(2,1)S(1)} %slice.51) | copy-start | bytes 6291460
  62.9 4.3 %copy-start.4 = (bf16[128,1024]{1,0:T(8,128)(2,1)S(1)}, bf16[128,1024]{1,0:T(8,128)(2,1)}, u32[]{:S(2)}) copy-start(bf16[128,1024]{1,0:T(8,128)(2,1)} %param.11) | copy-start | bytes 786436
  62.9 4.3 %copy-start.14 = (f32[1024]{0:T(1024)S(1)}, f32[1024]{0:T(1024)}, u32[]{:S(2)}) copy-start(f32[1024]{0:T(1024)} %param.14) | copy-start | bytes 12292
  67.2 2.7 %copy-start.1 = (bf16[12,256,1024]{2,1,0:T(8,128)(2,1)}, bf16[12,256,1024]{2,1,0:T(8,128)(2,1)S(1)}, u32[]{:S(2)}) copy-start(bf16[12,256,1024]{2,1,0:T(8,128)(2,1)S(1)} %slice.46) | copy-start | bytes 18874372
  70.9 3.3 %copy-start.10 = (bf16[1,128,1,8,128]{4,3,2,1,0:T(8,128)(2,1)}, bf16[1,128,1,8,128]{4,3,2,1,0:T(8,128)(2,1)S(1)}, u32[]{:S(2)}) copy-start(bf16[1,128,1,8,128]{4,3,2,1,0:T(8,128)(2,1)S(1)} %get-tuple-element.10) | copy-start | bytes 786436
  71.1 3.1 %copy-start.5 = (bf16[1,128,1,8,128]{1,4,3,2,0:T(8,128)(2,1)}, bf16[1,128,1,8,128]{1,4,3,2,0:T(8,128)(2,1)S(1)}, u32[]{:S(2)}) copy-start(bf16[1,128,1,8,128]{1,4,3,2,0:T(8,128)(2,1)S(1)} %copy.96) | copy-start | bytes 786436
  72.5 0.8 copy-start.8
  73.3 1.1 copy-start.16
  73.3 2.2 %copy-start = (bf16[1,1024,2048]{2,1,0:T(8,128)(2,1)S(1)}, bf16[1,1024,2048]{2,1,0:T(8,128)(2,1)}, u32[]{:S(2)}) copy-start(bf16[1,1024,2048]{2,1,0:T(8,128)(2,1)} %refs_1_.3) | copy-start | bytes 12582916
  119.4 0.8 copy-start.17
  119.8 0.8 copy-start.15
  120.6 44.6 %copy-start.13 = (f32[1,4,1024]{2,1,0:T(4,128)}, f32[1,4,1024]{2,1,0:T(4,128)S(1)}, u32[]{:S(2)}) copy-start(f32[1,4,1024]{2,1,0:T(4,128)S(1)} %fusion.10) | copy-start | bytes 49156
  165.1 1.6 copy-start.3
  166.7 5.6 %slice-start = ((s8[6291456]{0:T(1024)(128)(4,1)}), s8[2097152]{0:T(1024)(128)(4,1)S(1)}, s32[]{:S(2)}) async-start(s8[6291456]{0:T(1024)(128)(4,1)} %bitcast.96), calls=%async_computation | async-start | bytes 4194304
  169.7 1.6 copy-start.6
  169.7 1.6 copy-start.7
  169.7 1.6 copy-start.9
  169.7 1.9 %copy-start.12 = (bf16[1,128,1,8,128]{4,3,2,1,0:T(8,128)(2,1)S(1)}, bf16[1,128,1,8,128]{4,3,2,1,0:T(8,128)(2,1)}, u32[]{:S(2)}) copy-start(bf16[1,128,1,8,128]{4,3,2,1,0:T(8,128)(2,1)} %get-tuple-element.9) | copy-start | bytes 786436
  169.7 2.2 %copy-start.11 = (bf16[1,128,1,8,128]{4,3,2,1,0:T(8,128)(2,1)S(1)}, bf16[1,128,1,8,128]{4,3,2,1,0:T(8,128)(2,1)}, u32[]{:S(2)}) copy-start(bf16[1,128,1,8,128]{4,3,2,1,0:T(8,128)(2,1)} %copy-done.10) | copy-start | bytes 786436
  171.3 2.2 %slice-start.1 = ((s8[6291456]{0:T(1024)(128)(4,1)}), s8[4194304]{0:T(1024)(128)(4,1)S(1)}, s32[]{:S(2)}) async-start(s8[6291456]{0:T(1024)(128)(4,1)} %bitcast.96), calls=%async_computation.1 | async-start | bytes 8388608

commit v3 on v2

--- a/solution.py
+++ b/solution.py
@@ -39,8 +39,8 @@
         layer_norm(inputs, scale_gain).astype(jnp.bfloat16).reshape(row_count * length, model_width)
     )
     projected = lax.dot_general(
-        normed, weight[: 3 * model_width], NT, preferred_element_type=jnp.float32
-    ).astype(jnp.bfloat16)
+        normed, weight, NT, preferred_element_type=jnp.float32
+    ).astype(jnp.bfloat16)[:, : 3 * model_width]
     projected = projected.reshape(row_count, length, 3, head_count, head_width)
     queries = projected[:, :, 0]
     keys_all = projected[:, :, 1]
@@ -82,7 +82,7 @@
     return jnp.concatenate([rows[:, :half], rows[:, half:]], axis=0)
 
 
-def expert_kernel(chips, backward, groups_of, *refs):
+def expert_kernel(chips, backward, groups_of, order, *refs):
     if backward:
         rows_in, w1_hbm, w2_hbm, kept, rows_out = refs[:5]
         rest = refs[5:]
@@ -117,7 +117,7 @@
         )
 
     dispatch = {}
-    for k in range(chips - 1, 0, -1):
+    for k in order:
         dispatch[k] = remote(packed.at[peer_chip[k]], got_a.at[k], send_a.at[k], recv_a.at[k], peer[k])
         dispatch[k].start()
     across, over, back = {}, {}, {}
@@ -182,7 +182,7 @@
             to_pair[k] = fold(theirs).astype(jnp.bfloat16)
             over[k] = remote(to_pair.at[k], from_pair.at[k], send_c.at[k], recv_c.at[k], pair)
             over[k].start()
-        for k in reversed(group):
+        for k in group:
             over[k].wait_recv()
             total = fold(part[pl.ds(2 * cap * k, cap), :]) + from_pair[k].astype(jnp.float32)
             if k:
@@ -211,97 +211,139 @@
     core = lax.rem(rank, 2)
     side = lax.rem(lax.div(rank, 2), 2)
     line = lax.div(rank, 4)
-    there = [flip(line, k, lines) for k in range(lines)]
-
-    def name(k, x, c):
-        return there[k] * 4 + x * 2 + c
+
+    def name(shift, x, c):
+        return (line + shift) * 4 + x * 2 + c
 
     pair = {"expert": name(0, side, 1 - core)}
     x_peer = {"expert": name(0, 1 - side, core)}
     y_peer = {"groups": 1 - group, "expert": rank}
-    z_peer = [{"expert": name(k, side, core)} for k in range(lines)]
+    z_peer = {shift: {"expert": name(shift, side, core)} for shift in (-1, 1)}
+    exists = {-1: line > 0, 1: line < lines - 1}
     barrier = pltpu.get_barrier_semaphore()
-    for target in [pair, x_peer, y_peer] + z_peer[1:]:
+    around = [
+        {"expert": lax.rem(line + turn, lines) * 4 + side * 2 + core} for turn in (1, lines - 1)
+    ]
+    for target in [pair, x_peer, y_peer] + around:
         pl.semaphore_signal(barrier, inc=1, device_id=target, device_id_type=MESH)
-    pl.semaphore_wait(barrier, lines + 2)
+    pl.semaphore_wait(barrier, 5)
 
     mine = (group * half, half)
     other = ((1 - group) * half, half)
-    started = []
-
-    def copy(kind, k, target, shard, columns, source=None):
+    ends = (other[0] + quarter, quarter)
+
+    def slot(shift):
+        return 0 if shift == 0 else 2 * abs(shift) - (1 if shift < 0 else 0)
+
+    def copy(kind, shift, target, shard, columns, source=None):
         place = pl.ds(pl.multiple_of(columns[0], quarter), columns[1])
         dst = out.at[shard, :, place]
         src = dst if source is None else source.at[:, place]
+        at = slot(shift)
         return pltpu.make_async_remote_copy(
-            src_ref=src, dst_ref=dst, send_sem=send.at[kind, k], recv_sem=recv.at[kind, k],
+            src_ref=src, dst_ref=dst, send_sem=send.at[kind, at], recv_sem=recv.at[kind, at],
             device_id=target, device_id_type=MESH,
         )
 
     def go(*args):
-        made = copy(*args)
-        made.start()
-        started.append(made)
-
-    ahead = side, core
+        copy(*args).start()
+
+    def landed(kind, shift, shard, columns):
+        copy(kind, shift, pair, shard, columns).wait_recv()
+
+    def sent(kind, shift, columns):
+        copy(kind, shift, pair, rank, columns).wait_send()
+
+    def present(shift):
+        return line + shift >= 0 if shift < 0 else line + shift < lines
+
     keep = pltpu.make_async_copy(own, out.at[rank], local_sem)
     keep.start()
     go(1, 0, x_peer, rank, mine, own)
-    for k in range(1, lines):
-        go(0, k, z_peer[k], rank, mine, own)
-    go(4, 0, x_peer, rank, (other[0] + quarter, quarter), own)
+    for step in (-1, 1):
+        @pl.when(exists[step])
+        def _(step=step):
+            go(0, -step, z_peer[step], rank, mine, own)
+    go(4, 0, x_peer, rank, ends, own)
     go(5, 0, pair, rank, (0, width), own)
 
-    def landed(kind, k, shard, columns):
-        copy(kind, k, pair, shard, columns).wait_recv()
-
-    def first(k):
-        shard = name(k, *ahead)
-        landed(0, k, shard, mine)
-        go(1, k, x_peer, shard, mine)
-        go(2, k, y_peer, shard, mine)
-        go(5, k, pair, shard, mine)
-
-    def second(k):
-        if k:
-            shard = name(k, *ahead)
-            landed(2, k, shard, other)
-            go(4, k, x_peer, shard, (other[0] + quarter, quarter))
-            go(7, k, pair, shard, other)
-        shard = name(k, 1 - side, core)
-        landed(1, k, shard, mine)
-        go(3, k, y_peer, shard, (mine[0], quarter))
-        go(6, k, pair, shard, mine)
-
-    def third(k):
-        shard = name(k, 1 - side, core)
-        landed(4, k, shard, (other[0] + quarter, quarter))
-        go(9, k, pair, shard, (other[0] + quarter, quarter))
-        landed(3, k, shard, (other[0], quarter))
-        go(8, k, pair, shard, (other[0], quarter))
-
-    second(0)
-    for k in range(1, lines):
-        first(k)
-        if k > 1:
-            second(k - 1)
-        third(k - 1)
-    second(lines - 1)
-    third(lines - 1)
-
-    for k in range(lines):
-        shard = name(k, side, 1 - core)
-        across = name(k, 1 - side, 1 - core)
-        if k:
-            landed(5, k, shard, mine)
-            landed(7, k, shard, other)
+    def first(shift):
+        shard = name(shift, side, core)
+        landed(0, shift, shard, mine)
+        step = 1 if shift < 0 else -1
+        if abs(shift) < lines - 1:
+            @pl.when(exists[step])
+            def _():
+                go(0, shift - step, z_peer[step], shard, mine)
+        go(1, shift, x_peer, shard, mine)
+        go(2, shift, y_peer, shard, mine)
+        go(5, shift, pair, shard, mine)
+
+    def second(shift):
+        if shift:
+            shard = name(shift, side, core)
+            landed(2, shift, shard, other)
+            go(4, shift, x_peer, shard, ends)
+            go(7, shift, pair, shard, other)
+        shard = name(shift, 1 - side, core)
+        landed(1, shift, shard, mine)
+        go(3, shift, y_peer, shard, (mine[0], quarter))
+        go(6, shift, pair, shard, mine)
+
+    def third(shift):
+        shard = name(shift, 1 - side, core)
+        landed(4, shift, shard, ends)
+        go(9, shift, pair, shard, ends)
+        landed(3, shift, shard, (other[0], quarter))
+        go(8, shift, pair, shard, (other[0], quarter))
+
+    def last(shift):
+        shard = name(shift, side, 1 - core)
+        across = name(shift, 1 - side, 1 - core)
+        if shift:
+            landed(5, shift, shard, mine)
+            landed(7, shift, shard, other)
+            for kind in (2, 7):
+                sent(kind, shift, mine)
+            sent(5, shift, mine)
+            step = 1 if shift < 0 else -1
+            if abs(shift) < lines - 1:
+                @pl.when(exists[step])
+                def _():
+                    sent(0, shift - step, mine)
         else:
             landed(5, 0, shard, (0, width))
-        landed(6, k, across, mine)
-        landed(8, k, across, (other[0], quarter))
-        landed(9, k, across, (other[0] + quarter, quarter))
-    for made in started:
-        made.wait_send()
+            sent(5, 0, (0, width))
+            for step in (-1, 1):
+                @pl.when(exists[step])
+                def _(step=step):
+                    sent(0, -step, mine)
+        landed(6, shift, across, mine)
+        landed(8, shift, across, (other[0], quarter))
+        landed(9, shift, across, ends)
+        for kind in (1, 6):
+            sent(kind, shift, mine)
+        for kind in (3, 4, 8, 9):
+            sent(kind, shift, ends)
+
+    def both(stage, distance):
+        if distance == 0:
+            stage(0)
+            return
+        for shift in (-distance, distance):
+            @pl.when(present(shift))
+            def _(shift=shift):
+                stage(shift)
+
+    for distance in range(1, lines + 2):
+        if distance < lines:
+            both(first, distance)
+        if distance - 1 < lines:
+            both(second, distance - 1)
+        if distance >= 2:
+            both(third, distance - 2)
+    for distance in range(lines):
+        both(last, distance)
     keep.wait()
 
 
@@ -314,8 +356,8 @@
         out_specs=pl.BlockSpec(memory_space=pltpu.HBM),
         scratch_shapes=[
             pltpu.SemaphoreType.DMA,
-            pltpu.SemaphoreType.DMA((10, lines)),
-            pltpu.SemaphoreType.DMA((10, lines)),
+            pltpu.SemaphoreType.DMA((10, 2 * lines - 1)),
+            pltpu.SemaphoreType.DMA((10, 2 * lines - 1)),
         ],
         compiler_params=pltpu.CompilerParams(collective_id=2, has_side_effects=True),
         name="gather_weight",
@@ -327,7 +369,9 @@
     backward = kept is not None
     rows = 2 * rows_in.shape[0]
     width, hidden = expert_in.shape[1:]
-    groups_of = [list(range(chips // 2)), list(range(chips // 2, chips))]
+    part = chips // 4
+    groups_of = [list(range(i * part, (i + 1) * part)) for i in (0, 2, 3, 1)]
+    order = groups_of[1] + groups_of[2] + groups_of[3] + groups_of[0][1:]
     vmem = pl.BlockSpec(memory_space=pltpu.VMEM)
     hbm = pl.BlockSpec(memory_space=pltpu.HBM)
     message = jax.ShapeDtypeStruct(rows_in.shape, jnp.float32)
@@ -335,7 +379,7 @@
     block = pltpu.VMEM((chips, rows // chips, width // 2), jnp.bfloat16)
     sems = pltpu.SemaphoreType.DMA((chips,))
     return pl.pallas_call(
-        functools.partial(expert_kernel, chips, backward, groups_of),
+        functools.partial(expert_kernel, chips, backward, groups_of, order),
         out_shape=message if backward else (message, kept_shape),
         in_specs=[vmem, hbm, hbm] + ([vmem] if backward else []),
         out_specs=vmem if backward else (vmem, vmem),

time: 176 us -> 160 us (0.909)
  Pallas kernels: 138 us -> 124 us
  local copies, waits for them, and re-layouts: 17 us -> 9.57 us
  matrix products: 12.4 us -> 18.3 us
  other arithmetic: 7.18 us -> 5.28 us
    dot_general x2, matrix products: 3.35 us -> 11.1 us  [attend(): lax.dot_general(normed, weight, NT, preferred_element_type=jnp.float32)]
    pallas_call x2, Pallas kernels: 87.5 us -> 80.1 us  [run_experts(): pl.pallas_call(functools.partial(expert_kernel, chips, backward, groups_o...]
    pallas_call x1, Pallas kernels: 50.1 us -> 44.2 us  [gather_weight(): pl.pallas_call(functools.partial(gather_kernel, devices), out_shape=jax.S...]
    slice x2 -> x1, local copies, waits for them, and re-layouts: 4.47 us -> 0.21 us  [the longest x1 4.26 us: attend(): weight[:3 * model_width]]
    unnamed x44 -> x45, local copies, waits for them, and re-layouts: 6.9 us -> 6.79 us
where the time goes in v3:
time: 160 us; the launch traced here: 159 us
  Pallas kernels  124 us (78%)
  matrix products  18.3 us (11%)
  local copies, waits for them, and re-layouts  9.57 us (6%)
  other arithmetic  5.28 us (3%)
  between operations  1.8 us (1%)
    pallas_call x2, Pallas kernels, run_experts(): pl.pallas_call(functools.partial(expert_kernel, chips, backward, groups_o...  80.1 us
    pallas_call x1, Pallas kernels, gather_weight(): pl.pallas_call(functools.partial(gather_kernel, devices), out_shape=jax.S...  44.2 us
    dot_general x2, matrix products, attend(): lax.dot_general(normed, weight, NT, preferred_element_type=jnp.float32)  11.1 us
    unnamed x45, local copies, waits for them, and re-layouts  6.79 us

profile of v3, /device:TPU:0, one launch (start us, length us, event | category | flops | bytes accessed | tf_op | source)
XLA Modules:
  0.0 159.3 jit_solution(16758070748033464031)
XLA Ops:
  0.6 1.1 convert_reduce_fusion
  1.7 1.2 fusion.17
  2.9 2.1 %copy.73 = bf16[1024,256]{0,1:T(8,128)(2,1)} copy(bf16[1024,256]{1,0:T(8,128)(2,1)} %param.15) | data formatting | bytes 1048576 | tf_op args[4]
  5.0 44.2 %gather_weight.1 = bf16[16,256,1024]{2,1,0:T(8,128)(2,1)} custom-call(bf16[256,1024]{1,0:T(8,128)(2,1)} %bitcast.100), custom_call_target="tpu_custom_call" | custom-call | tf_op jit(solution)/shard_map/gather_weight/pallas_call | solution.py:352
  49.2 6.3 %fusion.28 = bf16[128,4096]{1,0:T(8,128)(2,1)S(1)} fusion(bf16[4096,1024]{1,0:T(8,128)(2,1)} %bitcast.94, bf16[128,1024]{1,0:T(8,128)(2,1)S(1)} %copy-done.2, f32[1024]{0:T(1024)S(1)} %copy-done.16, f32[128]{0:T(128)S(1)} %fusion.72, f32[128]{0:T(128)S(1)} %broadcast_multiply_fusion.1), kind=kOutput, calls=%fused_computation.58 | convolution fusion | flops 1074397184 | bytes 9704448 | tf_op jit(solution)/shard_map/dot_general | solution.py:41
  56.7 0.3 multiply_reduce_fusion.3
  57.6 0.4 copy-done.7
  58.1 1.8 %slice.47 = bf16[4,256,1024]{2,1,0:T(8,128)(2,1)S(1)} slice(bf16[16,256,1024]{2,1,0:T(8,128)(2,1)} %gather_weight.1), slice={[12:16], [0:256], [0:1024]} | slice | bytes 4194304 | tf_op jit(solution)/shard_map/slice | solution.py:59
  59.8 0.9 fusion.79
  61.3 0.8 reduce-window.6
  62.8 0.4 fusion.27.refs_0_
  63.2 2.2 %copy-done = bf16[1,1024,2048]{2,1,0:T(8,128)(2,1)S(1)} copy-done((bf16[1,1024,2048]{2,1,0:T(8,128)(2,1)S(1)}, bf16[1,1024,2048]{2,1,0:T(8,128)(2,1)}, u32[]{:S(2)}) %copy-start) | copy-done | bytes 4194328
  65.4 38.6 %experts.1 = (f32[320,1024]{1,0:T(8,128)S(1)}, bf16[640,2048]{1,0:T(8,128)(2,1)S(1)}) custom-call(f32[320,1024]{1,0:T(8,128)S(1)} %fusion.27.refs_0_, bf16[1,1024,2048]{2,1,0:T(8,128)(2,1)S(1)} %copy-done, bf16[1,2048,1024]{2,1,0:T(8,128)(2,1)} %refs_2_.3), custom_call_target="tpu_custom_call" | custom-call | flops 5368709120 | bytes 20971520 | tf_op jit(solution)/shard_map/experts/pallas_call | solution.py:381
  104.0 0.4 convolution_multiply_fusion.3
  104.4 0.4 fusion.2
  104.9 0.4 fusion.9
  105.3 0.6 multiply_convert_fusion.1
  106.0 0.3 fusion.21.refs_0_
  106.3 0.3 copy-done.1
  106.6 41.5 %experts_back.1 = f32[320,1024]{1,0:T(8,128)S(1)} custom-call(f32[320,1024]{1,0:T(8,128)S(1)} %fusion.21.refs_0_, bf16[1,1024,2048]{2,1,0:T(8,128)(2,1)S(1)} %copy-done.1, bf16[1,2048,1024]{2,1,0:T(8,128)(2,1)} %refs_2_.3, bf16[640,2048]{1,0:T(8,128)(2,1)S(1)} %get-tuple-element.5.refs_3_), custom_call_target="tpu_custom_call" | custom-call | flops 5368709120 | bytes 20971520 | tf_op jit(solution)/shard_map/experts_back/pallas_call | solution.py:381
  148.1 0.4 multiply_reduce_fusion.1
  148.6 0.3 fusion.77
  148.8 0.8 copy-done.3
  149.7 0.5 convolution_convert_fusion.5
  150.4 1.5 fusion.6
  151.9 0.3 multiply_reduce_fusion
  152.2 0.3 fusion.7
  152.5 0.3 copy-done.10
  152.8 0.3 fusion.8
  153.2 4.8 %fusion.20 = (f32[128]{0:T(128)S(1)}, f32[128,1024]{1,0:T(8,128)S(1)}) fusion(bf16[128,1024]{1,0:T(8,128)(2,1)S(1)} %copy-done.2, f32[128]{0:T(128)S(1)} %broadcast_multiply_fusion.1, f32[1024]{0:T(1024)S(1)} %copy-done.16, bf16[4096,1024]{1,0:T(8,128)(2,1)} %bitcast.95, bf16[128,3072]{0,1:T(8,128)(2,1)S(1)} %bitcast.98), kind=kOutput, calls=%fused_computation.39 | convolution fusion | flops 1074659200 | bytes 9966592 | tf_op jit(solution)/shard_map/transpose(jvp())/dot_general | solution.py:41
  158.0 0.3 fusion.76
  158.3 1.0 add_convert_fusion
  (71 shorter events, 2.8 us)
Async XLA Ops:
  5.0 44.2 %copy-start.2 = (bf16[128,1024]{1,0:T(8,128)(2,1)S(1)}, bf16[128,1024]{1,0:T(8,128)(2,1)}, u32[]{:S(2)}) copy-start(bf16[128,1024]{1,0:T(8,128)(2,1)} %param.11) | copy-start | bytes 786436
  5.0 44.2 %copy-start.16 = (f32[1024]{0:T(1024)S(1)}, f32[1024]{0:T(1024)}, u32[]{:S(2)}) copy-start(f32[1024]{0:T(1024)} %param.14) | copy-start | bytes 12292
  55.5 1.1 copy-start.17
  55.9 1.2 copy-start.9
  55.9 1.7 %copy-start.11 = (bf16[1,128,1,8,128]{4,3,2,1,0:T(8,128)(2,1)}, bf16[1,128,1,8,128]{4,3,2,1,0:T(8,128)(2,1)S(1)}, u32[]{:S(2)}) copy-start(bf16[1,128,1,8,128]{4,3,2,1,0:T(8,128)(2,1)S(1)} %get-tuple-element.10) | copy-start | bytes 786436
  57.1 0.9 copy-start.7
  57.3 0.7 copy-start.5
  59.8 1.2 copy-start.18
  59.8 2.9 %copy-start.15 = (f32[1024]{0:T(1024)S(1)}, f32[1024]{0:T(1024)}, u32[]{:S(2)}) copy-start(f32[1024]{0:T(1024)} %param.16) | copy-start | bytes 12292
  63.2 2.2 %copy-start = (bf16[1,1024,2048]{2,1,0:T(8,128)(2,1)S(1)}, bf16[1,1024,2048]{2,1,0:T(8,128)(2,1)}, u32[]{:S(2)}) copy-start(bf16[1,1024,2048]{2,1,0:T(8,128)(2,1)} %refs_1_.3) | copy-start | bytes 12582916
  65.4 38.6 %copy-start.19 = (f32[128,2]{0,1:T(2,128)S(1)}, f32[128,2]{0,1:T(2,128)}, u32[]{:S(2)}) copy-start(f32[128,2]{0,1:T(2,128)} %param.18) | copy-start | bytes 3076
  104.4 0.9 copy-start.14
  104.4 2.2 %copy-start.1 = (bf16[1,1024,2048]{2,1,0:T(8,128)(2,1)S(1)}, bf16[1,1024,2048]{2,1,0:T(8,128)(2,1)}, u32[]{:S(2)}) copy-start(bf16[1,1024,2048]{2,1,0:T(8,128)(2,1)} %refs_1_.3) | copy-start | bytes 12582916
  105.3 42.8 %copy-start.13 = (f32[1,4,1024]{2,1,0:T(4,128)}, f32[1,4,1024]{2,1,0:T(4,128)S(1)}, u32[]{:S(2)}) copy-start(f32[1,4,1024]{2,1,0:T(4,128)S(1)} %fusion.9) | copy-start | bytes 49156
  148.8 0.9 copy-start.3
  150.2 1.7 %copy-start.6 = (bf16[1,128,1,8,128]{1,4,3,2,0:T(8,128)(2,1)S(1)}, bf16[1,128,1,8,128]{1,4,3,2,0:T(8,128)(2,1)}, u32[]{:S(2)}) copy-start(bf16[1,128,1,8,128]{1,4,3,2,0:T(8,128)(2,1)} %copy-done.5) | copy-start | bytes 786436
  150.2 1.7 %copy-start.8 = (f32[8,128,128]{1,2,0:T(8,128)S(1)}, f32[8,128,128]{1,2,0:T(8,128)}, u32[]{:S(2)}) copy-start(f32[8,128,128]{1,2,0:T(8,128)} %copy-done.7) | copy-start | bytes 1572868
  150.2 2.0 %copy-start.12 = (bf16[1,128,1,8,128]{4,3,2,1,0:T(8,128)(2,1)S(1)}, bf16[1,128,1,8,128]{4,3,2,1,0:T(8,128)(2,1)}, u32[]{:S(2)}) copy-start(bf16[1,128,1,8,128]{4,3,2,1,0:T(8,128)(2,1)} %copy-done.11) | copy-start | bytes 786436
  151.9 1.0 copy-start.10
  153.2 5.1 %copy-start.4 = (f32[128,1024]{1,0:T(8,128)S(1)}, f32[128,1024]{1,0:T(8,128)}, u32[]{:S(2)}) copy-start(f32[128,1024]{1,0:T(8,128)} %copy-done.3) | copy-start | bytes 1572868

commit v4 on v3

--- a/solution.py
+++ b/solution.py
@@ -96,6 +96,7 @@
     chip = lax.div(rank, 2)
     pair = 2 * chip + (1 - core)
     cap = packed.shape[1] // 2
+    spot = {k: i for i, k in enumerate(sum(groups_of, []))}
     load_1 = pltpu.make_async_copy(w1_hbm.at[0], w1, w_sem.at[0])
     load_2 = pltpu.make_async_copy(w2_hbm.at[0], w2, w_sem.at[1])
     load_1.start()
@@ -135,12 +136,12 @@
             across[k].wait_recv()
             mine = got_a[k] if k else packed[chip]
             rows = jnp.concatenate([unfold(mine), unfold(got_b[k])], axis=0)
-            x_ref[pl.ds(2 * cap * k, 2 * cap), :] = rows.astype(jnp.bfloat16)
+            x_ref[pl.ds(2 * cap * spot[k], 2 * cap), :] = rows.astype(jnp.bfloat16)
         if not w_ready:
             load_1.wait()
             load_2.wait()
             w_ready = True
-        first, count = 2 * cap * group[0], 2 * cap * len(group)
+        first, count = 2 * cap * spot[group[0]], 2 * cap * len(group)
         block = pl.ds(first, count)
         hidden = h_scr.shape[1]
         width = part.shape[1]
@@ -178,13 +179,13 @@
 
         lax.fori_loop(0, width // TILE, out_tile, 0)
         for k in group:
-            theirs = part[pl.ds(2 * cap * k + cap, cap), :]
+            theirs = part[pl.ds(2 * cap * spot[k] + cap, cap), :]
             to_pair[k] = fold(theirs).astype(jnp.bfloat16)
             over[k] = remote(to_pair.at[k], from_pair.at[k], send_c.at[k], recv_c.at[k], pair)
             over[k].start()
         for k in group:
             over[k].wait_recv()
-            total = fold(part[pl.ds(2 * cap * k, cap), :]) + from_pair[k].astype(jnp.float32)
+            total = fold(part[pl.ds(2 * cap * spot[k], cap), :]) + from_pair[k].astype(jnp.float32)
             if k:
                 to_back[k] = total.astype(jnp.bfloat16)
                 back[k] = remote(to_back.at[k], out.at[chip], send_d.at[k], recv_d.at[k], peer[k])
@@ -370,8 +371,9 @@
     rows = 2 * rows_in.shape[0]
     width, hidden = expert_in.shape[1:]
     part = chips // 4
-    groups_of = [list(range(i * part, (i + 1) * part)) for i in (0, 2, 3, 1)]
-    order = groups_of[1] + groups_of[2] + groups_of[3] + groups_of[0][1:]
+    near, side, far, last = [list(range(i * part, (i + 1) * part)) for i in range(4)]
+    groups_of = [near + far, last + side] if backward else [near, far, last, side]
+    order = far + last + side + near[1:]
     vmem = pl.BlockSpec(memory_space=pltpu.VMEM)
     hbm = pl.BlockSpec(memory_space=pltpu.HBM)
     message = jax.ShapeDtypeStruct(rows_in.shape, jnp.float32)

time: 160 us -> 158 us (0.988)
    pallas_call x2, Pallas kernels: 80.1 us -> 78.4 us  [run_experts(): pl.pallas_call(functools.partial(expert_kernel, chips, backward, groups_o...]
where the time goes in v4:
time: 158 us
  Pallas kernels  123 us (78%)
  matrix products  18.3 us (12%)
  local copies, waits for them, and re-layouts  9.57 us (6%)
  other arithmetic  5.28 us (3%)
  between operations  1.8 us (1%)
    pallas_call x2, Pallas kernels, run_experts(): pl.pallas_call(functools.partial(expert_kernel, chips, backward, groups_o...  78.4 us
    pallas_call x1, Pallas kernels, gather_weight(): pl.pallas_call(functools.partial(gather_kernel, devices), out_shape=jax.S...  44.2 us
    dot_general x2, matrix products, attend(): lax.dot_general(normed, weight, NT, preferred_element_type=jnp.float32)  11.1 us
    unnamed x45, local copies, waits for them, and re-layouts  6.79 us

profile of v4, /device:TPU:0, one launch (start us, length us, event | category | flops | bytes accessed | tf_op | source)
XLA Modules:
  0.0 157.6 jit_solution(13269249076230871380)
XLA Ops:
  0.6 1.1 convert_reduce_fusion
  1.7 1.2 fusion.17
  2.9 2.1 %copy.73 = bf16[1024,256]{0,1:T(8,128)(2,1)} copy(bf16[1024,256]{1,0:T(8,128)(2,1)} %param.15) | data formatting | bytes 1048576 | tf_op args[4]
  5.0 44.2 %gather_weight.1 = bf16[16,256,1024]{2,1,0:T(8,128)(2,1)} custom-call(bf16[256,1024]{1,0:T(8,128)(2,1)} %bitcast.100), custom_call_target="tpu_custom_call" | custom-call | tf_op jit(solution)/shard_map/gather_weight/pallas_call | solution.py:353
  49.2 6.3 %fusion.28 = bf16[128,4096]{1,0:T(8,128)(2,1)S(1)} fusion(bf16[4096,1024]{1,0:T(8,128)(2,1)} %bitcast.94, bf16[128,1024]{1,0:T(8,128)(2,1)S(1)} %copy-done.2, f32[1024]{0:T(1024)S(1)} %copy-done.16, f32[128]{0:T(128)S(1)} %fusion.72, f32[128]{0:T(128)S(1)} %broadcast_multiply_fusion.1), kind=kOutput, calls=%fused_computation.58 | convolution fusion | flops 1074397184 | bytes 9704448 | tf_op jit(solution)/shard_map/dot_general | solution.py:41
  56.7 0.3 multiply_reduce_fusion.3
  57.6 0.4 copy-done.7
  58.1 1.8 %slice.47 = bf16[4,256,1024]{2,1,0:T(8,128)(2,1)S(1)} slice(bf16[16,256,1024]{2,1,0:T(8,128)(2,1)} %gather_weight.1), slice={[12:16], [0:256], [0:1024]} | slice | bytes 4194304 | tf_op jit(solution)/shard_map/slice | solution.py:59
  59.8 0.9 fusion.79
  61.3 0.8 reduce-window.6
  62.8 0.4 fusion.27.refs_0_
  63.2 2.2 %copy-done = bf16[1,1024,2048]{2,1,0:T(8,128)(2,1)S(1)} copy-done((bf16[1,1024,2048]{2,1,0:T(8,128)(2,1)S(1)}, bf16[1,1024,2048]{2,1,0:T(8,128)(2,1)}, u32[]{:S(2)}) %copy-start) | copy-done | bytes 4194328
  65.4 38.6 %experts.1 = (f32[320,1024]{1,0:T(8,128)S(1)}, bf16[640,2048]{1,0:T(8,128)(2,1)S(1)}) custom-call(f32[320,1024]{1,0:T(8,128)S(1)} %fusion.27.refs_0_, bf16[1,1024,2048]{2,1,0:T(8,128)(2,1)S(1)} %copy-done, bf16[1,2048,1024]{2,1,0:T(8,128)(2,1)} %refs_2_.3), custom_call_target="tpu_custom_call" | custom-call | flops 5368709120 | bytes 20971520 | tf_op jit(solution)/shard_map/experts/pallas_call | solution.py:383
  104.0 0.4 convolution_multiply_fusion.3
  104.4 0.4 fusion.2
  104.9 0.4 fusion.9
  105.3 0.6 multiply_convert_fusion.1
  106.0 0.3 fusion.21.refs_0_
  106.3 0.3 copy-done.1
  106.6 39.8 %experts_back.1 = f32[320,1024]{1,0:T(8,128)S(1)} custom-call(f32[320,1024]{1,0:T(8,128)S(1)} %fusion.21.refs_0_, bf16[1,1024,2048]{2,1,0:T(8,128)(2,1)S(1)} %copy-done.1, bf16[1,2048,1024]{2,1,0:T(8,128)(2,1)} %refs_2_.3, bf16[640,2048]{1,0:T(8,128)(2,1)S(1)} %get-tuple-element.5.refs_3_), custom_call_target="tpu_custom_call" | custom-call | flops 5368709120 | bytes 20971520 | tf_op jit(solution)/shard_map/experts_back/pallas_call | solution.py:383
  146.4 0.4 multiply_reduce_fusion.1
  146.9 0.3 fusion.77
  147.1 0.8 copy-done.3
  148.0 0.5 convolution_convert_fusion.5
  148.7 1.5 fusion.6
  150.2 0.3 multiply_reduce_fusion
  150.5 0.3 fusion.7
  150.8 0.3 copy-done.10
  151.1 0.3 fusion.8
  151.5 4.8 %fusion.20 = (f32[128]{0:T(128)S(1)}, f32[128,1024]{1,0:T(8,128)S(1)}) fusion(bf16[128,1024]{1,0:T(8,128)(2,1)S(1)} %copy-done.2, f32[128]{0:T(128)S(1)} %broadcast_multiply_fusion.1, f32[1024]{0:T(1024)S(1)} %copy-done.16, bf16[4096,1024]{1,0:T(8,128)(2,1)} %bitcast.95, bf16[128,3072]{0,1:T(8,128)(2,1)S(1)} %bitcast.98), kind=kOutput, calls=%fused_computation.39 | convolution fusion | flops 1074659200 | bytes 9966592 | tf_op jit(solution)/shard_map/transpose(jvp())/dot_general | solution.py:41
  156.3 0.3 fusion.76
  156.6 1.0 add_convert_fusion
  (71 shorter events, 2.8 us)
Async XLA Ops:
  5.0 44.2 %copy-start.2 = (bf16[128,1024]{1,0:T(8,128)(2,1)S(1)}, bf16[128,1024]{1,0:T(8,128)(2,1)}, u32[]{:S(2)}) copy-start(bf16[128,1024]{1,0:T(8,128)(2,1)} %param.11) | copy-start | bytes 786436
  5.0 44.2 %copy-start.16 = (f32[1024]{0:T(1024)S(1)}, f32[1024]{0:T(1024)}, u32[]{:S(2)}) copy-start(f32[1024]{0:T(1024)} %param.14) | copy-start | bytes 12292
  55.5 1.1 copy-start.17
  55.9 1.2 copy-start.9
  55.9 1.7 %copy-start.11 = (bf16[1,128,1,8,128]{4,3,2,1,0:T(8,128)(2,1)}, bf16[1,128,1,8,128]{4,3,2,1,0:T(8,128)(2,1)S(1)}, u32[]{:S(2)}) copy-start(bf16[1,128,1,8,128]{4,3,2,1,0:T(8,128)(2,1)S(1)} %get-tuple-element.10) | copy-start | bytes 786436
  57.1 0.9 copy-start.7
  57.3 0.7 copy-start.5
  59.8 1.2 copy-start.18
  59.8 2.9 %copy-start.15 = (f32[1024]{0:T(1024)S(1)}, f32[1024]{0:T(1024)}, u32[]{:S(2)}) copy-start(f32[1024]{0:T(1024)} %param.16) | copy-start | bytes 12292
  63.2 2.2 %copy-start = (bf16[1,1024,2048]{2,1,0:T(8,128)(2,1)S(1)}, bf16[1,1024,2048]{2,1,0:T(8,128)(2,1)}, u32[]{:S(2)}) copy-start(bf16[1,1024,2048]{2,1,0:T(8,128)(2,1)} %refs_1_.3) | copy-start | bytes 12582916
  65.4 38.6 %copy-start.19 = (f32[128,2]{0,1:T(2,128)S(1)}, f32[128,2]{0,1:T(2,128)}, u32[]{:S(2)}) copy-start(f32[128,2]{0,1:T(2,128)} %param.18) | copy-start | bytes 3076
  104.4 0.9 copy-start.14
  104.4 2.2 %copy-start.1 = (bf16[1,1024,2048]{2,1,0:T(8,128)(2,1)S(1)}, bf16[1,1024,2048]{2,1,0:T(8,128)(2,1)}, u32[]{:S(2)}) copy-start(bf16[1,1024,2048]{2,1,0:T(8,128)(2,1)} %refs_1_.3) | copy-start | bytes 12582916
  105.3 41.1 %copy-start.13 = (f32[1,4,1024]{2,1,0:T(4,128)}, f32[1,4,1024]{2,1,0:T(4,128)S(1)}, u32[]{:S(2)}) copy-start(f32[1,4,1024]{2,1,0:T(4,128)S(1)} %fusion.9) | copy-start | bytes 49156
  147.1 0.9 copy-start.3
  148.5 1.7 %copy-start.6 = (bf16[1,128,1,8,128]{1,4,3,2,0:T(8,128)(2,1)S(1)}, bf16[1,128,1,8,128]{1,4,3,2,0:T(8,128)(2,1)}, u32[]{:S(2)}) copy-start(bf16[1,128,1,8,128]{1,4,3,2,0:T(8,128)(2,1)} %copy-done.5) | copy-start | bytes 786436
  148.5 1.7 %copy-start.8 = (f32[8,128,128]{1,2,0:T(8,128)S(1)}, f32[8,128,128]{1,2,0:T(8,128)}, u32[]{:S(2)}) copy-start(f32[8,128,128]{1,2,0:T(8,128)} %copy-done.7) | copy-start | bytes 1572868
  148.5 2.0 %copy-start.12 = (bf16[1,128,1,8,128]{4,3,2,1,0:T(8,128)(2,1)S(1)}, bf16[1,128,1,8,128]{4,3,2,1,0:T(8,128)(2,1)}, u32[]{:S(2)}) copy-start(bf16[1,128,1,8,128]{4,3,2,1,0:T(8,128)(2,1)} %copy-done.11) | copy-start | bytes 786436
  150.2 1.0 copy-start.10
  151.5 5.1 %copy-start.4 = (f32[128,1024]{1,0:T(8,128)S(1)}, f32[128,1024]{1,0:T(8,128)}, u32[]{:S(2)}) copy-start(f32[128,1024]{1,0:T(8,128)} %copy-done.3) | copy-start | bytes 1572868
